TPU v7x, 256 devices: a whole 4x4x8 slice. The times are simulated.
256 devices in a mesh: rep: 4 (over x_lo, core), ctx: 64 (over z, y, x_hi).
Axes of the slice: x: 4 (x_hi: 2, x_lo: 2; x = x_hi * 2 + x_lo), y: 4, z: 8, core: 2. Of those that a mesh axis runs over, the one named last changes fastest.
Arguments:
- grad_out: bfloat16 [4, 2048, 8192], P('rep', None, 'ctx'), may hold values from -6 to 6
- gate: bfloat16 [4, 2048, 8192], P('rep', None, 'ctx'), may hold values from -6 to 6
- values: bfloat16 [4, 2048, 8192], P('rep', None, 'ctx'), may hold values from -6 to 6
- filters: float32 [2048, 8192], P('ctx'), may hold values from -0.0625 to 0.0625
- skip: float32 [2048], P('ctx'), may hold values from 0.5 to 1.5
Outputs:
- d_values: bfloat16 [4, 2048, 8192], P('rep', None, 'ctx')
- d_gate: bfloat16 [4, 2048, 8192], P('rep', None, 'ctx')
- d_filter: float32 [2048, 8192], P('ctx')
All inputs are finite; a program needn't handle non-finite values.
Results may differ from a plain program's by a relative error of at most 0.005.
Values may be sent and summed in bfloat16 or wider, within the bound.
A program may use at most 64 MiB of HBM per device.

v0:
```python
import math

import jax
import jax.numpy as jnp
from jax import lax
from jax.sharding import PartitionSpec as P


def dft_table(length):
    counter = lax.iota(jnp.int32, length)
    product = counter[:, None] * counter[None, :] % length
    angle = product.astype(jnp.float32) * (2.0 * math.pi / length)
    return (jnp.cos(angle), -jnp.sin(angle))


def twist_table(first_size, second_size):
    total = first_size * second_size
    product = (
        lax.iota(jnp.int32, first_size)[:, None] * lax.iota(jnp.int32, second_size)[None, :] % total
    )
    angle = product.astype(jnp.float32) * (2.0 * math.pi / total)
    return (jnp.cos(angle), -jnp.sin(angle))


def contract(spec, left, right):
    return jnp.einsum(
        spec, left, right, precision=lax.Precision.HIGHEST, preferred_element_type=jnp.float32
    )


def build_tables(tokens_here, ctx_count):
    first_cos, first_sin = dft_table(tokens_here)
    second_cos, second_sin = dft_table(2 * ctx_count)
    twist_cos, twist_sin = twist_table(tokens_here, 2 * ctx_count)
    half = tokens_here // 2
    first_fwd = jnp.stack([first_cos[:, :half], first_sin[:, :half]])
    second_fwd = jnp.stack(
        [jnp.stack([second_cos, second_sin]), jnp.stack([-second_sin, second_cos])]
    )
    second_inv = jnp.stack(
        [jnp.stack([second_cos, -second_sin]), jnp.stack([second_sin, second_cos])]
    )
    rows_cos = first_cos[:half]
    rows_sin = first_sin[:half]
    first_inv = jnp.stack([jnp.stack([rows_cos, -rows_sin]), jnp.stack([rows_sin, rows_cos])])
    return (first_fwd, second_fwd, second_inv, first_inv, twist_cos, twist_sin)


def forward_real(signal, tables):
    first_fwd, second_fwd, second_inv, first_inv, twist_cos, twist_sin = tables
    channels = signal.shape[0]
    half = first_fwd.shape[2]
    grid = signal.astype(jnp.float32).reshape(channels, half, second_fwd.shape[2])
    section = contract("pkn,cnq->pckq", first_fwd, grid)
    turned = jnp.stack(
        [
            section[0] * twist_cos - section[1] * twist_sin,
            section[0] * twist_sin + section[1] * twist_cos,
        ]
    )
    return contract("pckq,psqj->sckj", turned, second_fwd)


def inverse(spectrum, tables, with_imag):
    first_fwd, second_fwd, second_inv, first_inv, twist_cos, twist_sin = tables
    channels = spectrum.shape[1]
    half = first_fwd.shape[2]
    total = 2 * half * second_fwd.shape[2]
    back = contract("pckj,psjn->sckn", spectrum, second_inv)
    turned = jnp.stack(
        [back[0] * twist_cos + back[1] * twist_sin, back[1] * twist_cos - back[0] * twist_sin]
    )
    if with_imag:
        result = contract("pckq,psnk->scnq", turned, first_inv) / total
        return result.reshape(2, channels, total // 2)
    result = contract("pckq,pnk->cnq", turned, first_inv[:, 0]) / total
    return result.reshape(channels, total // 2)


def on_device(grad_out, gate, values, filters, skip):
    tokens_here = values.shape[2]
    ctx_count = lax.axis_size("ctx")
    seq_length = tokens_here * ctx_count
    tables = build_tables(tokens_here, ctx_count)
    grad_here, gate_here, value_here = (
        lax.all_to_all(grad_out, "ctx", split_axis=1, concat_axis=2, tiled=True),
        lax.all_to_all(gate, "ctx", split_axis=1, concat_axis=2, tiled=True),
        lax.all_to_all(values, "ctx", split_axis=1, concat_axis=2, tiled=True),
    )
    d_conv = (grad_here.astype(jnp.float32) * gate_here.astype(jnp.float32)).astype(jnp.bfloat16)
    d_conv = lax.optimization_barrier(d_conv)
    batch, width, seq_here = value_here.shape
    rows = batch * width
    value_rows = value_here.reshape(rows, seq_here)
    conv_rows = d_conv.reshape(rows, seq_here)
    filter_spec = forward_real(filters, tables)
    spectra = forward_real(jnp.concatenate([value_rows, conv_rows], axis=0), tables)
    filter_real = filter_spec[0]
    filter_imag = filter_spec[1]
    value_real = spectra[0, :rows]
    value_imag = spectra[1, :rows]
    conv_real = spectra[0, rows:]
    conv_imag = spectra[1, rows:]
    joined = jnp.stack(
        [
            filter_real * value_real
            - filter_imag * value_imag
            - (filter_real * conv_imag - filter_imag * conv_real),
            filter_real * value_imag
            + filter_imag * value_real
            + (filter_real * conv_real + filter_imag * conv_imag),
        ]
    )
    results = inverse(joined, tables, True)
    forward_conv = results[0]
    back_conv = results[1]
    value_f = value_rows.astype(jnp.float32)
    conv_f = conv_rows.astype(jnp.float32)
    skip_col = jnp.tile(skip, batch)[:, None]
    mixed = (forward_conv + skip_col * value_f).astype(jnp.bfloat16)
    mixed = lax.optimization_barrier(mixed)
    d_values_here = (
        (back_conv + skip_col * conv_f).astype(jnp.bfloat16).reshape(batch, width, seq_here)
    )
    mixed = mixed.reshape(batch, width, seq_here)
    second_out = (grad_here.astype(jnp.float32) * mixed.astype(jnp.float32)).astype(jnp.bfloat16)
    d_values, returned = (
        lax.all_to_all(d_values_here, "ctx", split_axis=2, concat_axis=1, tiled=True),
        lax.all_to_all(second_out, "ctx", split_axis=2, concat_axis=1, tiled=True),
    )
    cross = jnp.stack(
        [
            conv_real * value_real + conv_imag * value_imag,
            conv_imag * value_real - conv_real * value_imag,
        ]
    )
    factor = 1.0 / math.sqrt(lax.axis_size("rep") * seq_length)
    filter_part = inverse(cross, tables, False) * factor
    d_filter = lax.psum(filter_part, "rep")
    return (d_values, returned, d_filter)


def solution(mesh):
    placed = (
        P("rep", None, "ctx"),
        P("rep", None, "ctx"),
        P("rep", None, "ctx"),
        P("ctx", None),
        P("ctx"),
    )
    return jax.shard_map(
        on_device,
        mesh=mesh,
        in_specs=placed,
        out_specs=(P("rep", None, "ctx"), P("rep", None, "ctx"), P("ctx", None)),
        check_vma=False,
    )
```

profile of v0, /device:TPU:1, one launch (start us, length us, event | category | flops | bytes accessed | tf_op | source)
XLA Modules:
  0.0 367.5 jit_solution(5299224357162759332)
XLA Ops:
  9.5 11.4 %reduce.1 = bf16[2048,128]{1,0:T(8,128)(2,1)S(1)} reduce(bf16[2048,1,128]{2,1,0:T(2,128)(2,1)S(1)} %bitcast.218, bf16[]{:T(256)} %broadcast.234), dimensions={1}, to_apply=%bitcast.202.reduce_sub_computation | reduce | bytes 1048578
  21.8 15.3 %all-to-all-start.1 = ((bf16[64,2,2048]{2,1,0:T(2,128)(2,1)}), bf16[64,2,2048]{2,1,0:T(2,128)(2,1)S(1)}, u32[]{:S(2)}, u32[]{:S(2)}) async-start(bf16[64,2,2048]{2,1,0:T(2,128)(2,1)} %reshape.221), calls=%async_computation.1 | async-start | bytes 1048576 | tf_op jit(solution)/shard_map/all_to_all | solution.py:86
  37.1 8.1 %copy.214 = bf16[1,2048,128]{2,0,1:T(2,128)(2,1)S(1)} copy(bf16[1,2048,128]{2,1,0:T(8,128)(2,1)S(1)} %copy-done.15) | data formatting | bytes 1048576 | tf_op args[1]
  45.3 11.4 %reduce = bf16[2048,128]{1,0:T(8,128)(2,1)S(1)} reduce(bf16[2048,1,128]{2,1,0:T(2,128)(2,1)S(1)} %bitcast.221, bf16[]{:T(256)} %broadcast.234), dimensions={1}, to_apply=%bitcast.201.reduce_sub_computation | reduce | bytes 1048578
  59.5 11.6 %reduce.2 = bf16[2048,128]{1,0:T(8,128)(2,1)S(1)} reduce(bf16[2048,1,128]{2,1,0:T(2,128)(2,1)S(1)} %bitcast.222, bf16[]{:T(256)} %broadcast.234), dimensions={1}, to_apply=%bitcast.203.reduce_sub_computation | reduce | bytes 1048578
  74.0 12.7 %all-to-all-start.2 = ((bf16[64,2,2048]{2,1,0:T(2,128)(2,1)}), bf16[64,2,2048]{2,1,0:T(2,128)(2,1)S(1)}, u32[]{:S(2)}, u32[]{:S(2)}) async-start(bf16[64,2,2048]{2,1,0:T(2,128)(2,1)} %reshape.219), calls=%async_computation.2 | async-start | bytes 1048576 | tf_op jit(solution)/shard_map/all_to_all | solution.py:87
  91.0 5.5 %fusion.18 = f32[2,32,128,128]{2,3,1,0:T(8,128)} fusion(f32[1,2,128,128]{2,3,0,1:T(8,128)S(1)} %get-tuple-element.21, f32[1,2,128,128]{2,3,0,1:T(8,128)S(1)} %get-tuple-element.28, f32[1,32,128,128]{3,2,1,0:T(8,128)S(1)} %get-tuple-element.13, f32[1,32,128,128]{3,2,1,0:T(8,128)S(1)} %get-tuple-element.12), kind=kOutput, calls=%fused_computation.26 | convolution fusion | flops 3222339584 | bytes 8650752 | tf_op jit(solution)/shard_map/pckq,psqj->sckj/dot_general | solution.py:26
  96.5 6.1 %all-to-all-done.2 = bf16[64,2,2048]{2,1,0:T(2,128)(2,1)S(1)} async-done(((bf16[64,2,2048]{2,1,0:T(2,128)(2,1)}), bf16[64,2,2048]{2,1,0:T(2,128)(2,1)S(1)}, u32[]{:S(2)}, u32[]{:S(2)}) %all-to-all-start.2) | async-done | bytes 524320 | tf_op jit(solution)/shard_map/all_to_all | solution.py:87
  102.7 7.7 %all-to-all-start = ((bf16[64,2,2048]{2,1,0:T(2,128)(2,1)}), bf16[64,2,2048]{2,1,0:T(2,128)(2,1)S(1)}, u32[]{:S(2)}, u32[]{:S(2)}) async-start(bf16[64,2,2048]{2,1,0:T(2,128)(2,1)} %reshape.223), calls=%async_computation | async-start | bytes 1048576 | tf_op jit(solution)/shard_map/all_to_all | solution.py:88
  113.4 12.4 %all-to-all-done = bf16[64,2,2048]{2,1,0:T(2,128)(2,1)S(1)} async-done(((bf16[64,2,2048]{2,1,0:T(2,128)(2,1)}), bf16[64,2,2048]{2,1,0:T(2,128)(2,1)S(1)}, u32[]{:S(2)}, u32[]{:S(2)}) %all-to-all-start) | async-done | bytes 524320 | tf_op jit(solution)/shard_map/all_to_all | solution.py:88
  133.0 9.2 %fusion.17 = f32[2,64,128,128]{2,3,1,0:T(8,128)S(1)} fusion(f32[1,64,128,128]{2,3,0,1:T(8,128)S(1)} %get-tuple-element.6, f32[1,64,128,128]{2,3,0,1:T(8,128)S(1)} %get-tuple-element.5, f32[1,2,128,128]{2,3,0,1:T(8,128)S(1)} %get-tuple-element.21, f32[1,2,128,128]{2,3,0,1:T(8,128)S(1)} %copy-done.3), kind=kOutput, calls=%fused_computation.25 | convolution fusion | flops 6444613632 | bytes 17039360 | tf_op jit(solution)/shard_map/pckq,psqj->sckj/dot_general | solution.py:26
  145.9 7.1 %fusion.21 = f32[2,32,128,128]{3,2,1,0:T(8,128)S(1)} fusion(f32[1,32,128,128]{2,3,1,0:T(8,128)S(1)} %get-tuple-element.4, f32[1,32,128,128]{2,3,1,0:T(8,128)S(1)} %get-tuple-element.3, f32[1,2,128,128]{2,3,1,0:T(8,128)S(1)} %get-tuple-element.29, f32[1,2,128,128]{2,3,1,0:T(8,128)S(1)} %get-tuple-element.20), kind=kOutput, calls=%fused_computation.27 | convolution fusion | flops 3222339584 | bytes 8650752 | tf_op jit(solution)/shard_map/pckj,psjn->sckn/dot_general | solution.py:26
  153.0 7.3 %fusion.24 = f32[2,32,128,128]{3,2,1,0:T(8,128)S(1)} fusion(f32[1,32,128,128]{2,3,1,0:T(8,128)S(1)} %multiply_subtract_fusion.2, f32[1,32,128,128]{2,3,1,0:T(8,128)S(1)} %get-tuple-element.7, f32[1,2,128,128]{2,3,1,0:T(8,128)S(1)} %get-tuple-element.29, f32[1,2,128,128]{2,3,1,0:T(8,128)S(1)} %get-tuple-element.20), kind=kOutput, calls=%fused_computation.28 | convolution fusion | flops 3222339584 | bytes 8650752 | tf_op jit(solution)/shard_map/pckj,psjn->sckn/dot_general | solution.py:26
  169.7 6.7 %copy.122 = bf16[1,32,8192]{1,0,2:T(2,128)(2,1)} copy(bf16[1,32,8192]{2,1,0:T(8,128)(2,1)S(1)} %fusion.41) | data formatting | bytes 1048576 | tf_op jit(solution)/shard_map/convert_element_type | solution.py:126
  176.5 45.1 %reduce.4 = bf16[8192,32]{1,0:T(8,128)(2,1)S(1)} reduce(bf16[8192,1,32]{2,1,0:T(2,128)(2,1)} %bitcast.207, bf16[]{:T(256)} %broadcast.234), dimensions={1}, to_apply=%bitcast.183.reduce_sub_computation | reduce | bytes 1048578
  224.3 8.0 %all-to-all-start.4 = ((bf16[64,2,2048]{2,1,0:T(2,128)(2,1)}), bf16[64,2,2048]{2,1,0:T(2,128)(2,1)S(1)}, u32[]{:S(2)}, u32[]{:S(2)}) async-start(bf16[64,2,2048]{2,1,0:T(2,128)(2,1)} %reshape.227), calls=%async_computation.4 | async-start | bytes 1048576 | tf_op jit(solution)/shard_map/all_to_all | solution.py:129
  234.0 6.7 %copy.118 = bf16[1,32,8192]{1,0,2:T(2,128)(2,1)} copy(bf16[1,32,8192]{2,1,0:T(8,128)(2,1)S(1)} %add_convert_fusion) | data formatting | bytes 1048576 | tf_op jit(solution)/shard_map/convert_element_type | solution.py:123
  240.7 45.1 %reduce.3 = bf16[8192,32]{1,0:T(8,128)(2,1)S(1)} reduce(bf16[8192,1,32]{2,1,0:T(2,128)(2,1)} %bitcast.206, bf16[]{:T(256)} %broadcast.234), dimensions={1}, to_apply=%bitcast.181.reduce_sub_computation | reduce | bytes 1048578
  288.6 12.3 %all-to-all-start.3 = ((bf16[64,2,2048]{2,1,0:T(2,128)(2,1)}), bf16[64,2,2048]{2,1,0:T(2,128)(2,1)S(1)}, u32[]{:S(2)}, u32[]{:S(2)}) async-start(bf16[64,2,2048]{2,1,0:T(2,128)(2,1)} %reshape.225), calls=%async_computation.3 | async-start | bytes 1048576 | tf_op jit(solution)/shard_map/all_to_all | solution.py:128
  307.4 7.2 %reshape.228 = bf16[8192,1,32]{2,1,0:T(2,128)(2,1)} reshape(bf16[64,2,2048]{2,1,0:T(2,128)(2,1)S(1)} %all-to-all-done.4) | data formatting | bytes 1048576
  314.6 8.0 %copy.123 = bf16[1,32,8192]{2,1,0:T(8,128)(2,1)S(1)} copy(bf16[1,32,8192]{1,0,2:T(2,128)(2,1)} %bitcast.208) | data formatting | bytes 1048576 | tf_op jit(solution)/shard_map/all_to_all | solution.py:129
  323.9 7.2 %reshape.226 = bf16[8192,1,32]{2,1,0:T(2,128)(2,1)} reshape(bf16[64,2,2048]{2,1,0:T(2,128)(2,1)S(1)} %all-to-all-done.3) | data formatting | bytes 1048576
  331.0 8.0 %copy.119 = bf16[1,32,8192]{2,1,0:T(8,128)(2,1)S(1)} copy(bf16[1,32,8192]{1,0,2:T(2,128)(2,1)} %bitcast.209) | data formatting | bytes 1048576 | tf_op jit(solution)/shard_map/all_to_all | solution.py:128
  340.3 17.8 %all-reduce.2.cloned.1.call-done = f32[32,8192]{1,0:T(8,128)} async-done(((f32[32,8192]{1,0:T(8,128)}), f32[32,8192]{1,0:T(8,128)}) %all-reduce.2.cloned.1.call-update) | async-done | bytes 1048592 | tf_op jit(solution)/shard_map/psum | solution.py:139
  (99 shorter events, 54.7 us)
Async XLA Ops:
  9.0 28.1 %copy-start.15 = (bf16[1,2048,128]{2,1,0:T(8,128)(2,1)S(1)}, bf16[1,2048,128]{2,1,0:T(8,128)(2,1)}, u32[]{:S(2)}) copy-start(bf16[1,2048,128]{2,1,0:T(8,128)(2,1)} %param.6) | copy-start | bytes 1572868
  21.8 52.1 %all-to-all-start.1 = ((bf16[64,2,2048]{2,1,0:T(2,128)(2,1)}), bf16[64,2,2048]{2,1,0:T(2,128)(2,1)S(1)}, u32[]{:S(2)}, u32[]{:S(2)}) async-start(bf16[64,2,2048]{2,1,0:T(2,128)(2,1)} %reshape.221), calls=%async_computation.1 | async-start | bytes 1048576 | tf_op jit(solution)/shard_map/all_to_all | solution.py:86
  57.6 14.5 %copy-start.6 = (f32[32,8192]{1,0:T(8,128)S(1)}, f32[32,8192]{1,0:T(8,128)}, u32[]{:S(2)}) copy-start(f32[32,8192]{1,0:T(8,128)} %param.8) | copy-start | bytes 3145732
  72.5 1.3 copy-start.11
  72.6 1.3 copy-start.13
  72.7 17.5 %copy-start.7 = (f32[128,128]{1,0:T(8,128)}, f32[128,128]{1,0:T(8,128)S(1)}, u32[]{:S(2)}) copy-start(f32[128,128]{1,0:T(8,128)S(1)} %copy.102) | copy-start | bytes 196612
  72.8 17.4 %copy-start.9 = (f32[128,128]{1,0:T(8,128)}, f32[128,128]{1,0:T(8,128)S(1)}, u32[]{:S(2)}) copy-start(f32[128,128]{1,0:T(8,128)S(1)} %copy.103) | copy-start | bytes 196612
  73.9 17.1 %copy-start.2 = (f32[1,2,128,128]{2,3,0,1:T(8,128)}, f32[1,2,128,128]{2,3,0,1:T(8,128)S(1)}, u32[]{:S(2)}) copy-start(f32[1,2,128,128]{2,3,0,1:T(8,128)S(1)} %get-tuple-element.28) | copy-start | bytes 393220
  73.9 16.2 %copy-start.16 = (f32[1,128,64]{1,2,0:T(8,128)}, f32[1,128,64]{1,2,0:T(8,128)S(1)}, u32[]{:S(2)}) copy-start(f32[1,128,64]{1,2,0:T(8,128)S(1)} %get-tuple-element.30) | copy-start | bytes 98308
  73.9 16.2 %copy-start.18 = (f32[1,128,64]{1,2,0:T(8,128)}, f32[1,128,64]{1,2,0:T(8,128)S(1)}, u32[]{:S(2)}) copy-start(f32[1,128,64]{1,2,0:T(8,128)S(1)} %get-tuple-element.31) | copy-start | bytes 98308
  74.0 28.7 %all-to-all-start.2 = ((bf16[64,2,2048]{2,1,0:T(2,128)(2,1)}), bf16[64,2,2048]{2,1,0:T(2,128)(2,1)S(1)}, u32[]{:S(2)}, u32[]{:S(2)}) async-start(bf16[64,2,2048]{2,1,0:T(2,128)(2,1)} %reshape.219), calls=%async_computation.2 | async-start | bytes 1048576 | tf_op jit(solution)/shard_map/all_to_all | solution.py:87
  102.7 23.1 %all-to-all-start = ((bf16[64,2,2048]{2,1,0:T(2,128)(2,1)}), bf16[64,2,2048]{2,1,0:T(2,128)(2,1)S(1)}, u32[]{:S(2)}, u32[]{:S(2)}) async-start(bf16[64,2,2048]{2,1,0:T(2,128)(2,1)} %reshape.223), calls=%async_computation | async-start | bytes 1048576 | tf_op jit(solution)/shard_map/all_to_all | solution.py:88
  127.5 3.5 copy-start.12
  127.5 3.5 copy-start.14
  131.1 1.9 copy-start.3
  142.2 2.2 copy-start
  153.0 7.4 %copy-start.8 = (f32[128,128]{1,0:T(8,128)S(1)}, f32[128,128]{1,0:T(8,128)}, u32[]{:S(2)}) copy-start(f32[128,128]{1,0:T(8,128)} %copy-done.7) | copy-start | bytes 196612
  153.0 7.4 %copy-start.10 = (f32[128,128]{1,0:T(8,128)S(1)}, f32[128,128]{1,0:T(8,128)}, u32[]{:S(2)}) copy-start(f32[128,128]{1,0:T(8,128)} %copy-done.9) | copy-start | bytes 196612
  160.3 3.5 copy-start.4
  160.4 3.5 copy-start.5
  166.2 1.1 copy-start.20
  224.3 64.2 %all-to-all-start.4 = ((bf16[64,2,2048]{2,1,0:T(2,128)(2,1)}), bf16[64,2,2048]{2,1,0:T(2,128)(2,1)S(1)}, u32[]{:S(2)}, u32[]{:S(2)}) async-start(bf16[64,2,2048]{2,1,0:T(2,128)(2,1)} %reshape.227), calls=%async_computation.4 | async-start | bytes 1048576 | tf_op jit(solution)/shard_map/all_to_all | solution.py:129
  288.6 35.3 %all-to-all-start.3 = ((bf16[64,2,2048]{2,1,0:T(2,128)(2,1)}), bf16[64,2,2048]{2,1,0:T(2,128)(2,1)S(1)}, u32[]{:S(2)}, u32[]{:S(2)}) async-start(bf16[64,2,2048]{2,1,0:T(2,128)(2,1)} %reshape.225), calls=%async_computation.3 | async-start | bytes 1048576 | tf_op jit(solution)/shard_map/all_to_all | solution.py:128
  300.8 57.3 %all-reduce.2.cloned.1.call-start = ((), (), s32[]{:S(2)}) async-start(), calls=%async_computation.5 | async-start | bytes 2097152 | tf_op jit(solution)/shard_map/psum | solution.py:139
  (3 other events, 3.1 us)
Sparse Core Ops, SparseCore 0:
  307.5 50.5 all-reduce.1
where the time goes:
time: 373 us; the launch traced here: 367 us
  other arithmetic  138 us (37%)
  local copies, waits for them, and re-layouts  79.3 us (21%)
  starting transfers between devices  55.9 us (15%)
  matrix products  43.2 us (12%)
  waiting for transfers between devices  36.4 us (10%)
  between operations  14.9 us (4%)
    unnamed x5, other arithmetic  125 us
    unnamed x63, local copies, waits for them, and re-layouts  44.1 us
    dot_general x8, matrix products, contract(): jnp.einsum(spec, left, right, precision=lax.Precision.HIGHEST, preferred_...  43.2 us
    psum x1, waiting for transfers between devices, on_device(): d_filter = lax.psum(filter_part, 'rep')  17.8 us
    all_to_all x1, starting transfers between devices, on_device(): lax.all_to_all(grad_out, 'ctx', split_axis=1, concat_axis=2, tiled=True)  15.3 us
    all_to_all x1, starting transfers between devices, on_device(): lax.all_to_all(gate, 'ctx', split_axis=1, concat_axis=2, tiled=True)  12.7 us
    all_to_all x1, waiting for transfers between devices, on_device(): lax.all_to_all(values, 'ctx', split_axis=1, concat_axis=2, tiled=True)  12.4 us
    all_to_all x1, starting transfers between devices, on_device(): lax.all_to_all(d_values_here, 'ctx', split_axis=2, concat_axis=1, tiled=T...  12.3 us
  transfers between devices with their start and end apart: 6, of which 3 were waited for; matrix products, arithmetic and copies ran while one was open for 39% of the time, Pallas kernels for 0%

commit v1 on v0

v1 whole, which is shorter than its diff:
```python
import functools
import math

import jax
import jax.numpy as jnp
import ml_dtypes
import numpy as np
from jax import lax
from jax.experimental import pallas as pl
from jax.experimental.pallas import tpu as pltpu
from jax.sharding import PartitionSpec as P

F32 = jnp.float32
BF16 = jnp.bfloat16


def split_np(table):
    high = table.astype(ml_dtypes.bfloat16)
    low = (table - high.astype(np.float64)).astype(ml_dtypes.bfloat16)
    return high, low


@functools.lru_cache(None)
def tables(chunks, width):
    total = chunks * width
    n = np.arange(chunks)
    q = np.arange(width)
    outer = 2 * np.pi * np.outer(n + 0.25, n) / chunks
    turn = 2 * np.pi * np.outer(n + 0.25, q) / total
    inner = 2 * np.pi * (np.outer(q, q) % width) / width
    first = np.concatenate([np.cos(outer), -np.sin(outer)], axis=0)
    first_hi, first_lo = split_np(first)
    fwd_first = np.concatenate([first_hi, first_lo], axis=1)
    filter_first = np.concatenate([first_hi, first_hi, first_lo], axis=1)
    cos, sin = np.cos(inner), np.sin(inner)
    second = np.block([[cos, -sin], [sin, cos]])
    second_hi, second_lo = split_np(second)
    back_hi, back_lo = split_np(second.T)
    last = np.concatenate([np.cos(outer).T, -np.sin(outer).T], axis=1)
    last_hi, last_lo = split_np(last)
    zero = np.zeros_like(last_lo)
    inv_last = np.concatenate(
        [np.concatenate([last_hi, last_hi], axis=1), np.concatenate([last_lo, zero], axis=1)], axis=0
    )
    twist = np.stack([np.cos(turn), np.sin(turn)]).astype(np.float32)
    return fwd_first, filter_first, second_hi, second_lo, back_hi, back_lo, inv_last, twist


def dot(left, right):
    return jnp.dot(left, right, preferred_element_type=F32)


def split(array):
    high = array.astype(BF16)
    low = (array - high.astype(F32)).astype(BF16)
    return high, low


def dot3(left, right_hi, right_lo):
    high, low = split(left)
    return dot(high, right_hi) + (dot(low, right_hi) + dot(high, right_lo))


def pack_kernel(grad_ref, gate_ref, value_ref, out_ref):
    rows, width = grad_ref.shape
    groups = rows // 8
    d_conv = grad_ref[...].astype(F32) * gate_ref[...].astype(F32)
    value = value_ref[...].astype(F32)
    both = jnp.concatenate([value.reshape(groups, 8, width), d_conv.reshape(groups, 8, width)], axis=1)
    out_ref[...] = both.astype(BF16)


def unpack_kernel(back_ref, grad_ref, d_values_ref, d_gate_ref):
    groups, _, width = back_ref.shape
    back = back_ref[...].astype(F32)
    grad = grad_ref[...].astype(F32)
    mixed = back[:, :8].reshape(groups * 8, width)
    d_values_ref[...] = back[:, 8:].reshape(groups * 8, width).astype(BF16)
    d_gate_ref[...] = (grad * mixed).astype(BF16)


def conv_kernel(
    reps, chunks, width,
    skip_ref, data_ref, filter_ref,
    first_ref, filter_first_ref, second_hi_ref, second_lo_ref, back_hi_ref, back_lo_ref, last_ref, twist_ref,
    out_ref, d_filter_ref,
    rows_in, rows_out, filter_rows, filter_spec, cross, spectra,
):
    here = 8
    mine = lax.axis_index("rep") * here
    scale = 1.0 / (chunks * width)

    def twisted(section):
        cos, sin = twist_ref[0], twist_ref[1]
        real, imag = section[:chunks], section[chunks:]
        return jnp.concatenate([real * cos + imag * sin, imag * cos - real * sin], axis=1)

    def untwisted(section):
        cos, sin = twist_ref[0], twist_ref[1]
        real, imag = section[:, :width], section[:, width:]
        return jnp.concatenate([real * cos - imag * sin, imag * cos + real * sin], axis=0)

    for n in range(chunks):
        filter_rows[n * here:(n + 1) * here, :] = filter_ref[pl.ds(mine, here), n * width:(n + 1) * width]

    @pl.loop(0, here)
    def _(c):
        high, low = split(filter_rows[pl.ds(c, chunks, stride=here), :])
        section = dot(filter_first_ref[...], jnp.concatenate([high, low, high], axis=0))
        filter_spec[c] = dot3(twisted(section), second_hi_ref[...], second_lo_ref[...]) * scale
        cross[c] = jnp.zeros((chunks, 2 * width), F32)

    @pl.loop(0, reps)
    def _(r):
        rows_in[...] = data_ref[:, r].astype(F32).reshape(chunks * 16, width)

        @pl.loop(0, here)
        def _(c):
            value = rows_in[pl.ds(c, chunks, stride=16), :].astype(BF16)
            d_conv = rows_in[pl.ds(c + here, chunks, stride=16), :].astype(BF16)
            pair = jnp.concatenate([value, d_conv], axis=1)
            section = dot(first_ref[...], jnp.concatenate([pair, pair], axis=0))
            spectra[c] = jnp.concatenate([twisted(section[:, :width]), twisted(section[:, width:])], axis=0)

        flat = spectra[...].reshape(here * 2 * chunks, 2 * width)
        spectra[...] = dot3(flat, second_hi_ref[...], second_lo_ref[...]).reshape(spectra.shape)

        @pl.loop(0, here)
        def _(c):
            vr, vi = spectra[c, :chunks, :width], spectra[c, :chunks, width:]
            dr, di = spectra[c, chunks:, :width], spectra[c, chunks:, width:]
            fr, fi = filter_spec[c, :, :width], filter_spec[c, :, width:]
            cross[c, :, :width] += dr * vr + di * vi
            cross[c, :, width:] += di * vr - dr * vi
            spectra[c, :chunks, :width] = fr * vr - fi * vi
            spectra[c, :chunks, width:] = fr * vi + fi * vr
            spectra[c, chunks:, :width] = fr * dr + fi * di
            spectra[c, chunks:, width:] = fr * di - fi * dr

        flat = spectra[...].reshape(here * 2 * chunks, 2 * width)
        spectra[...] = dot3(flat, back_hi_ref[...], back_lo_ref[...]).reshape(spectra.shape)

        @pl.loop(0, here)
        def _(c):
            skip = skip_ref[mine + c]
            both = jnp.concatenate(
                [untwisted(spectra[c, :chunks]), untwisted(spectra[c, chunks:])], axis=1
            )
            high, low = split(both)
            parts = dot(last_ref[...], jnp.concatenate([high, low], axis=0))
            result = parts[:chunks] + parts[chunks:]
            value = rows_in[pl.ds(c, chunks, stride=16), :]
            d_conv = rows_in[pl.ds(c + here, chunks, stride=16), :]
            rows_out[pl.ds(c, chunks, stride=16), :] = result[:, :width] + skip * value
            rows_out[pl.ds(c + here, chunks, stride=16), :] = result[:, width:] + skip * d_conv

        out_ref[:, r] = rows_out[...].reshape(chunks, 16, width).astype(BF16)

    factor = scale / math.sqrt(reps * chunks * width)

    @pl.loop(0, here)
    def _(c):
        both = untwisted(dot3(cross[c] * factor, back_hi_ref[...], back_lo_ref[...]))
        high, low = split(both)
        parts = dot(last_ref[...], jnp.concatenate([high, low], axis=0))
        filter_rows[pl.ds(c, chunks, stride=here), :] = parts[:chunks] + parts[chunks:]

    for n in range(chunks):
        d_filter_ref[:, n * width:(n + 1) * width] = filter_rows[n * here:(n + 1) * here, :]


def on_device(grad_out, gate, values, filters, skip):
    reps = lax.axis_size("rep")
    chunks = lax.axis_size("ctx")
    channels, width = values.shape[1:]
    groups = channels // 8
    vmem = pl.BlockSpec(memory_space=pltpu.VMEM)
    smem = pl.BlockSpec(memory_space=pltpu.SMEM)
    params = pltpu.CompilerParams(vmem_limit_bytes=56 * 1024 * 1024)
    grad_out, gate, values = grad_out[0], gate[0], values[0]
    packed = pl.pallas_call(
        pack_kernel,
        out_shape=jax.ShapeDtypeStruct((groups, 16, width), BF16),
        in_specs=[vmem] * 3,
        out_specs=vmem,
        compiler_params=params,
        name="pack",
    )(grad_out, gate, values)
    rows = lax.all_to_all(packed, ("ctx", "rep"), split_axis=0, concat_axis=0, tiled=True)
    rows = rows.reshape(chunks, reps, 16, width)
    consts = [jnp.asarray(t) for t in tables(chunks, width)]
    results, d_filter = pl.pallas_call(
        functools.partial(conv_kernel, reps, chunks, width),
        out_shape=[
            jax.ShapeDtypeStruct((chunks, reps, 16, width), BF16),
            jax.ShapeDtypeStruct((8, chunks * width), F32),
        ],
        in_specs=[smem] + [vmem] * (2 + len(consts)),
        out_specs=[vmem, vmem],
        scratch_shapes=[
            pltpu.VMEM((chunks * 16, width), F32),
            pltpu.VMEM((chunks * 16, width), F32),
            pltpu.VMEM((chunks * 8, width), F32),
            pltpu.VMEM((8, chunks, 2 * width), F32),
            pltpu.VMEM((8, chunks, 2 * width), F32),
            pltpu.VMEM((8, 2 * chunks, 2 * width), F32),
        ],
        compiler_params=params,
        name="conv",
    )(skip, rows, filters, *consts)
    results = results.reshape(groups, 16, width)
    back = lax.all_to_all(results, ("ctx", "rep"), split_axis=0, concat_axis=0, tiled=True)
    d_filter = lax.all_gather(d_filter, "rep", axis=0, tiled=True)
    d_values, d_gate = pl.pallas_call(
        unpack_kernel,
        out_shape=[jax.ShapeDtypeStruct((channels, width), BF16)] * 2,
        in_specs=[vmem] * 2,
        out_specs=[vmem] * 2,
        compiler_params=params,
        name="unpack",
    )(back, grad_out)
    return d_values[None], d_gate[None], d_filter


def solution(mesh):
    placed = (
        P("rep", None, "ctx"),
        P("rep", None, "ctx"),
        P("rep", None, "ctx"),
        P("ctx", None),
        P("ctx"),
    )
    return jax.shard_map(
        on_device,
        mesh=mesh,
        in_specs=placed,
        out_specs=(P("rep", None, "ctx"), P("rep", None, "ctx"), P("ctx", None)),
        check_vma=False,
    )
```

time: 373 us -> 134 us (0.36); the launches traced: 367 us -> 133 us
  other arithmetic: 138 us -> 0 us
  local copies, waits for them, and re-layouts: 79.3 us -> 1.94 us
  starting transfers between devices: 55.9 us -> 6.55 us
  blocking collectives: 0 us -> 46.3 us
  matrix products: 43.2 us -> 0 us
  Pallas kernels: 0 us -> 33.1 us
  waiting for transfers between devices: 36.4 us -> 31.4 us
    unnamed x5 -> x0, other arithmetic: 125 us -> none
    all_to_all x5 -> x1, starting transfers between devices: 55.9 us -> 6.5 us  [on_device(): lax.all_to_all(results, ('ctx', 'rep'), split_axis=0, concat_axis=0, tile...]
    all_to_all x0 -> x1, blocking collectives: none -> 46.3 us  [on_device(): lax.all_to_all(packed, ('ctx', 'rep'), split_axis=0, concat_axis=0, tiled...]
    dot_general x8 -> x0, matrix products: 43.2 us -> none  [contract(): jnp.einsum(spec, left, right, precision=lax.Precision.HIGHEST, preferred_...]
    unnamed x63 -> x5, local copies, waits for them, and re-layouts: 44.1 us -> 1.94 us
    pallas_call x0 -> x3, Pallas kernels: none -> 33.1 us  [the longest x1 28.2 us: on_device(): pl.pallas_call(functools.partial(conv_kernel, reps, chunks, width), out_s...]
    all_gather x0 -> x1, waiting for transfers between devices: none -> 30.7 us  [on_device(): d_filter = lax.all_gather(d_filter, 'rep', axis=0, tiled=True)]
    all_to_all x5 -> x1, waiting for transfers between devices: 18.5 us -> 0.01 us  [on_device(): lax.all_to_all(results, ('ctx', 'rep'), split_axis=0, concat_axis=0, tile...]
  transfers between devices with their start and end apart: 6 -> 2, of which waited for: 3 -> 1; matrix products, arithmetic and copies ran while one was open for 39% -> 0% of each run, Pallas kernels for 0% -> 0%
where the time goes in v1:
time: 134 us; the launch traced here: 133 us
  blocking collectives  46.3 us (35%)
  Pallas kernels  33.1 us (25%)
  waiting for transfers between devices  31.4 us (23%)
  between operations  14 us (10%)
  starting transfers between devices  6.55 us (5%)
  local copies, waits for them, and re-layouts  1.94 us (1%)
    all_to_all x1, blocking collectives, on_device(): lax.all_to_all(packed, ('ctx', 'rep'), split_axis=0, concat_axis=0, tiled...  46.3 us
    all_gather x1, waiting for transfers between devices, on_device(): d_filter = lax.all_gather(d_filter, 'rep', axis=0, tiled=True)  30.7 us
    pallas_call x1, Pallas kernels, on_device(): pl.pallas_call(functools.partial(conv_kernel, reps, chunks, width), out_s...  28.2 us
    all_to_all x1, starting transfers between devices, on_device(): lax.all_to_all(results, ('ctx', 'rep'), split_axis=0, concat_axis=0, tile...  6.5 us
  transfers between devices with their start and end apart: 2, of which 1 were waited for; matrix products, arithmetic and copies ran while one was open for 0% of the time, Pallas kernels for 0%

profile of v1, /device:TPU:1, one launch (start us, length us, event | category | flops | bytes accessed | tf_op | source)
XLA Modules:
  0.0 133.3 jit_solution(16381528626773907201)
XLA Ops:
  7.2 2.5 %pack.1 = bf16[256,16,128]{2,1,0:T(8,128)(2,1)} custom-call(bf16[2048,128]{1,0:T(8,128)(2,1)} %bitcast.8, bf16[2048,128]{1,0:T(8,128)(2,1)} %bitcast.11, bf16[2048,128]{1,0:T(8,128)(2,1)} %bitcast.12), custom_call_target="tpu_custom_call" | custom-call | tf_op jit(solution)/shard_map/pack/pallas_call | solution.py:181
  9.7 46.3 %all_to_all.10 = bf16[256,16,128]{2,1,0:T(8,128)(2,1)} all-to-all(bf16[256,16,128]{2,1,0:T(8,128)(2,1)} %pack.1), channel_id=1, replica_groups=mesh['rep'=4,'ctx'=64] {'ctx','rep'}, dimensions={0} | all-to-all | bytes 2097152 | tf_op jit(solution)/shard_map/all_to_all | solution.py:189
  56.0 28.2 %conv.1 = (bf16[64,4,16,128]{3,2,1,0:T(8,128)(2,1)}, f32[8,8192]{1,0:T(8,128)}) custom-call(f32[32]{0:T(128)} %skip_ref.1, bf16[64,4,16,128]{3,2,1,0:T(8,128)(2,1)} %bitcast.7, f32[32,8192]{1,0:T(8,128)} %filter_ref.1, bf16[128,128]{1,0:T(8,128)(2,1)} %constant.16.clone.first_ref, bf16[128,192]{1,0:T(8,128)(2,1)} %constant.17.clone.filter_first_ref, ...), custom_call_target="tpu_custom_call" | custom-call | tf_op jit(solution)/shard_map/conv/pallas_call | solution.py:192
  84.2 6.5 %all-to-all-start.1 = ((bf16[256,16,128]{2,1,0:T(8,128)(2,1)}), bf16[256,16,128]{2,1,0:T(8,128)(2,1)S(1)}, u32[]{:S(2)}, u32[]{:S(2)}) async-start(bf16[256,16,128]{2,1,0:T(8,128)(2,1)} %bitcast.10), calls=%async_computation.1 | async-start | bytes 2097152 | tf_op jit(solution)/shard_map/all_to_all | solution.py:212
  90.7 0.0 all-gather.2.cloned.1.call-start
  90.7 0.7 all-gather.2.cloned.1.call-update
  91.4 30.7 %all-gather.2.cloned.1.call-done = f32[32,8192]{1,0:T(8,128)} async-done(((f32[8,8192]{1,0:T(8,128)}), f32[32,8192]{1,0:T(8,128)}) %all-gather.2.cloned.1.call-update) | async-done | bytes 1048592 | tf_op jit(solution)/shard_map/all_gather | solution.py:213
  122.1 0.0 copy-start.1
  122.1 0.0 all-to-all-done.1.back_ref
  122.1 0.0 copy-start
  122.1 1.0 copy-done
  123.1 2.4 %unpack.1 = (bf16[2048,128]{1,0:T(8,128)(2,1)}, bf16[2048,128]{1,0:T(8,128)(2,1)}) custom-call(bf16[256,16,128]{2,1,0:T(8,128)(2,1)} %copy-done, bf16[2048,128]{1,0:T(8,128)(2,1)} %bitcast.9), custom_call_target="tpu_custom_call" | custom-call | tf_op jit(solution)/shard_map/unpack/pallas_call | solution.py:214
  125.5 0.0 copy-done.1
  125.5 1.0 copy.17
Async XLA Ops:
  84.2 37.9 %all-to-all-start.1 = ((bf16[256,16,128]{2,1,0:T(8,128)(2,1)}), bf16[256,16,128]{2,1,0:T(8,128)(2,1)S(1)}, u32[]{:S(2)}, u32[]{:S(2)}) async-start(bf16[256,16,128]{2,1,0:T(8,128)(2,1)} %bitcast.10), calls=%async_computation.1 | async-start | bytes 2097152 | tf_op jit(solution)/shard_map/all_to_all | solution.py:212
  90.7 31.4 %all-gather.2.cloned.1.call-start = ((), (), s32[]{:S(2)}) async-start(), calls=%async_computation.2 | async-start | bytes 1310720 | tf_op jit(solution)/shard_map/all_gather | solution.py:213
  122.1 3.4 %copy-start.1 = (f32[32,8192]{1,0:T(8,128)S(1)}, f32[32,8192]{1,0:T(8,128)}, u32[]{:S(2)}) copy-start(f32[32,8192]{1,0:T(8,128)} %all-gather.2.cloned.1.call-done) | copy-start | bytes 3145732
  122.1 1.0 copy-start
Sparse Core Ops, SparseCore 0:
  93.9 28.1 all-gather.1

commit v2 on v1

--- a/solution.py
+++ b/solution.py
@@ -10,6 +10,7 @@
 from jax.experimental.pallas import tpu as pltpu
 from jax.sharding import PartitionSpec as P
 
+MESH = pl.DeviceIdType.MESH
 F32 = jnp.float32
 BF16 = jnp.bfloat16
 
@@ -61,34 +62,41 @@
     return dot(high, right_hi) + (dot(low, right_hi) + dot(high, right_lo))
 
 
-def pack_kernel(grad_ref, gate_ref, value_ref, out_ref):
-    rows, width = grad_ref.shape
-    groups = rows // 8
-    d_conv = grad_ref[...].astype(F32) * gate_ref[...].astype(F32)
-    value = value_ref[...].astype(F32)
-    both = jnp.concatenate([value.reshape(groups, 8, width), d_conv.reshape(groups, 8, width)], axis=1)
-    out_ref[...] = both.astype(BF16)
-
-
-def unpack_kernel(back_ref, grad_ref, d_values_ref, d_gate_ref):
-    groups, _, width = back_ref.shape
-    back = back_ref[...].astype(F32)
-    grad = grad_ref[...].astype(F32)
-    mixed = back[:, :8].reshape(groups * 8, width)
-    d_values_ref[...] = back[:, 8:].reshape(groups * 8, width).astype(BF16)
-    d_gate_ref[...] = (grad * mixed).astype(BF16)
-
-
-def conv_kernel(
-    reps, chunks, width,
-    skip_ref, data_ref, filter_ref,
+def whole_kernel(
+    reps, chunks, width, grid,
+    skip_ref, grad_ref, gate_ref, value_ref, filter_ref,
     first_ref, filter_first_ref, second_hi_ref, second_lo_ref, back_hi_ref, back_lo_ref, last_ref, twist_ref,
-    out_ref, d_filter_ref,
-    rows_in, rows_out, filter_rows, filter_spec, cross, spectra,
+    d_values_ref, d_gate_ref, d_filter_ref,
+    send, recv, result_out, back, rows_in, rows_out, filter_rows, filter_spec, cross, spectra, note_out, note_in,
+    send_sem, recv_sem, back_send_sem, back_sem, filter_send_sem, filter_sem, note_send_sem, note_sem,
 ):
     here = 8
-    mine = lax.axis_index("rep") * here
+    nz, ny, nx = grid
+    rep = lax.axis_index("rep")
+    ctx = lax.axis_index("ctx")
+    z, y, x = ctx // (ny * nx), (ctx // nx) % ny, ctx % nx
+    mine = rep * here
     scale = 1.0 / (chunks * width)
+
+    def place(zz, yy, xx):
+        return (zz % nz) * (ny * nx) + (yy % ny) * nx + xx % nx
+
+    def along_row(step):
+        return rep, place(z + step // nx, y, x + step % nx)
+
+    def along_column(step):
+        return (rep + step // ny) % reps, place(z, y + step % ny, x)
+
+    def swing(step, size):
+        return (step + 1) // 2 * (2 * (step % 2) - 1) + size
+
+    def partner(step):
+        rest = step // nz
+        return place(z + swing(step % nz, nz), y + swing(rest // nx, ny), x + rest % nx)
+
+    def peer(phase):
+        base = (rep + phase // 2 * 2) % reps
+        return base + phase % 2 * (1 - base % 2 * 2)
 
     def twisted(section):
         cos, sin = twist_ref[0], twist_ref[1]
@@ -100,8 +108,52 @@
         real, imag = section[:, :width], section[:, width:]
         return jnp.concatenate([real * cos - imag * sin, imag * cos + real * sin], axis=0)
 
+    barrier = pltpu.get_barrier_semaphore()
+
+    @pl.loop(1, nz * nx)
+    def _(step):
+        pl.semaphore_signal(barrier, 1, device_id=along_row(step), device_id_type=MESH)
+
+    @pl.loop(1, reps * ny)
+    def _(step):
+        pl.semaphore_signal(barrier, 1, device_id=along_column(step), device_id_type=MESH)
+
+    @pl.loop(0, chunks)
+    def _(j):
+        value = value_ref[j].astype(F32)
+        d_conv = grad_ref[j].astype(F32) * gate_ref[j].astype(F32)
+        both = jnp.concatenate([value.reshape(reps, here, width), d_conv.reshape(reps, here, width)], axis=1)
+        send[j] = both.astype(BF16)
+
+    note_out[...] = jnp.zeros_like(note_out)
+    recv[0, ctx] = send[ctx, rep]
+    pl.semaphore_wait(barrier, nz * nx + reps * ny - 2)
+
+    def note(step):
+        return pltpu.make_async_remote_copy(
+            src_ref=note_out, dst_ref=note_in.at[rep * ny + y],
+            send_sem=note_send_sem, recv_sem=note_sem, device_id=along_column(step), device_id_type=MESH,
+        )
+
+    @pl.loop(1, reps * ny)
+    def _(step):
+        note(step).start()
+
     for n in range(chunks):
         filter_rows[n * here:(n + 1) * here, :] = filter_ref[pl.ds(mine, here), n * width:(n + 1) * width]
+
+    count = reps * ny - 1
+    pltpu.make_async_copy(note_in.at[pl.ds(0, count)], note_in.at[pl.ds(0, count)], note_sem).wait()
+    pltpu.make_async_copy(note_in.at[pl.ds(0, count)], note_in.at[pl.ds(0, count)], note_send_sem).wait()
+
+    @pl.loop(1, reps * chunks)
+    def _(step):
+        phase = step // chunks
+        i, j = peer(phase), partner(step % chunks)
+        pltpu.make_async_remote_copy(
+            src_ref=send.at[j, i], dst_ref=recv.at[phase, ctx],
+            send_sem=send_sem, recv_sem=recv_sem.at[phase], device_id=(i, j), device_id_type=MESH,
+        ).start()
 
     @pl.loop(0, here)
     def _(c):
@@ -110,9 +162,8 @@
         filter_spec[c] = dot3(twisted(section), second_hi_ref[...], second_lo_ref[...]) * scale
         cross[c] = jnp.zeros((chunks, 2 * width), F32)
 
-    @pl.loop(0, reps)
-    def _(r):
-        rows_in[...] = data_ref[:, r].astype(F32).reshape(chunks * 16, width)
+    def convolve(phase):
+        rows_in[...] = recv[phase].astype(F32).reshape(chunks * 16, width)
 
         @pl.loop(0, here)
         def _(c):
@@ -154,7 +205,27 @@
             rows_out[pl.ds(c, chunks, stride=16), :] = result[:, :width] + skip * value
             rows_out[pl.ds(c + here, chunks, stride=16), :] = result[:, width:] + skip * d_conv
 
-        out_ref[:, r] = rows_out[...].reshape(chunks, 16, width).astype(BF16)
+        result_out[phase] = rows_out[...].reshape(chunks, 16, width).astype(BF16)
+
+    def send_back(phase, start):
+        other = peer(phase)
+
+        @pl.loop(start, chunks)
+        def _(step):
+            j = partner(step)
+            pltpu.make_async_remote_copy(
+                src_ref=result_out.at[phase, j], dst_ref=back.at[ctx, rep],
+                send_sem=back_send_sem, recv_sem=back_sem.at[phase], device_id=(other, j), device_id_type=MESH,
+            ).start()
+
+    for phase in range(reps):
+        blocks = chunks - 1 if phase == 0 else chunks
+        arrived = recv.at[phase, pl.ds(0, blocks)]
+        pltpu.make_async_copy(arrived, arrived, recv_sem.at[phase]).wait()
+        convolve(phase)
+        if phase == 0:
+            back[ctx, rep] = result_out[0, ctx]
+        send_back(phase, 1 if phase == 0 else 0)
 
     factor = scale / math.sqrt(reps * chunks * width)
 
@@ -165,61 +236,91 @@
         parts = dot(last_ref[...], jnp.concatenate([high, low], axis=0))
         filter_rows[pl.ds(c, chunks, stride=here), :] = parts[:chunks] + parts[chunks:]
 
+    own = pl.ds(pl.multiple_of(mine, here), here)
     for n in range(chunks):
-        d_filter_ref[:, n * width:(n + 1) * width] = filter_rows[n * here:(n + 1) * here, :]
-
-
-def on_device(grad_out, gate, values, filters, skip):
+        d_filter_ref[own, n * width:(n + 1) * width] = filter_rows[n * here:(n + 1) * here, :]
+
+    filter_copies = []
+    for phase in range(1, reps):
+        filter_copies.append(pltpu.make_async_remote_copy(
+            src_ref=d_filter_ref.at[own], dst_ref=d_filter_ref.at[own],
+            send_sem=filter_send_sem.at[phase], recv_sem=filter_sem.at[phase],
+            device_id=(peer(phase), ctx), device_id_type=MESH,
+        ))
+        filter_copies[-1].start()
+
+    for half in range(reps // 2):
+        for phase in (2 * half, 2 * half + 1):
+            blocks = chunks - 1 if phase == 0 else chunks
+            arrived = recv.at[phase, pl.ds(0, blocks)]
+            pltpu.make_async_copy(arrived, arrived, back_sem.at[phase]).wait()
+        side = (rep // 2 + half) % 2
+        rows = pl.ds(pl.multiple_of(side * 16, 16), 16)
+
+        @pl.loop(0, chunks)
+        def _(k):
+            block = back[k, pl.ds(side * 2, 2)].astype(F32)
+            mixed = block[:, :here].reshape(16, width)
+            d_values_ref[k, rows] = block[:, here:].reshape(16, width).astype(BF16)
+            d_gate_ref[k, rows] = (grad_ref[k, rows].astype(F32) * mixed).astype(BF16)
+
+    for copy in filter_copies:
+        copy.wait()
+    sent = send.at[pl.ds(0, chunks - 1)]
+    rest = send.at[chunks - 1, pl.ds(0, reps - 1)]
+    for sem in (send_sem, back_send_sem):
+        pltpu.make_async_copy(sent, sent, sem).wait()
+        pltpu.make_async_copy(rest, rest, sem).wait()
+
+
+def on_device(grid, grad_out, gate, values, filters, skip):
     reps = lax.axis_size("rep")
     chunks = lax.axis_size("ctx")
     channels, width = values.shape[1:]
-    groups = channels // 8
     vmem = pl.BlockSpec(memory_space=pltpu.VMEM)
     smem = pl.BlockSpec(memory_space=pltpu.SMEM)
-    params = pltpu.CompilerParams(vmem_limit_bytes=56 * 1024 * 1024)
-    grad_out, gate, values = grad_out[0], gate[0], values[0]
-    packed = pl.pallas_call(
-        pack_kernel,
-        out_shape=jax.ShapeDtypeStruct((groups, 16, width), BF16),
-        in_specs=[vmem] * 3,
-        out_specs=vmem,
-        compiler_params=params,
-        name="pack",
-    )(grad_out, gate, values)
-    rows = lax.all_to_all(packed, ("ctx", "rep"), split_axis=0, concat_axis=0, tiled=True)
-    rows = rows.reshape(chunks, reps, 16, width)
+    grad_out, gate, values = (a.reshape(chunks, channels // chunks, width) for a in (grad_out, gate, values))
     consts = [jnp.asarray(t) for t in tables(chunks, width)]
-    results, d_filter = pl.pallas_call(
-        functools.partial(conv_kernel, reps, chunks, width),
+    rows = chunks * 16
+    blocks = (reps, chunks, 16, width)
+    blocks_back = (chunks, reps, 16, width)
+    d_values, d_gate, d_filter = pl.pallas_call(
+        functools.partial(whole_kernel, reps, chunks, width, grid),
         out_shape=[
-            jax.ShapeDtypeStruct((chunks, reps, 16, width), BF16),
-            jax.ShapeDtypeStruct((8, chunks * width), F32),
+            jax.ShapeDtypeStruct(values.shape, BF16),
+            jax.ShapeDtypeStruct(values.shape, BF16),
+            jax.ShapeDtypeStruct(filters.shape, F32),
         ],
-        in_specs=[smem] + [vmem] * (2 + len(consts)),
-        out_specs=[vmem, vmem],
+        in_specs=[smem] + [vmem] * (4 + len(consts)),
+        out_specs=[vmem] * 3,
         scratch_shapes=[
-            pltpu.VMEM((chunks * 16, width), F32),
-            pltpu.VMEM((chunks * 16, width), F32),
+            pltpu.VMEM(blocks_back, BF16),
+            pltpu.VMEM(blocks, BF16),
+            pltpu.VMEM(blocks, BF16),
+            pltpu.VMEM(blocks_back, BF16),
+            pltpu.VMEM((rows, width), F32),
+            pltpu.VMEM((rows, width), F32),
             pltpu.VMEM((chunks * 8, width), F32),
             pltpu.VMEM((8, chunks, 2 * width), F32),
             pltpu.VMEM((8, chunks, 2 * width), F32),
             pltpu.VMEM((8, 2 * chunks, 2 * width), F32),
+            pltpu.VMEM((8, width), F32),
+            pltpu.VMEM((reps * grid[1], 8, width), F32),
+            pltpu.SemaphoreType.DMA,
+            pltpu.SemaphoreType.DMA((reps,)),
+            pltpu.SemaphoreType.DMA,
+            pltpu.SemaphoreType.DMA((reps,)),
+            pltpu.SemaphoreType.DMA((reps,)),
+            pltpu.SemaphoreType.DMA((reps,)),
+            pltpu.SemaphoreType.DMA,
+            pltpu.SemaphoreType.DMA,
         ],
-        compiler_params=params,
-        name="conv",
-    )(skip, rows, filters, *consts)
-    results = results.reshape(groups, 16, width)
-    back = lax.all_to_all(results, ("ctx", "rep"), split_axis=0, concat_axis=0, tiled=True)
-    d_filter = lax.all_gather(d_filter, "rep", axis=0, tiled=True)
-    d_values, d_gate = pl.pallas_call(
-        unpack_kernel,
-        out_shape=[jax.ShapeDtypeStruct((channels, width), BF16)] * 2,
-        in_specs=[vmem] * 2,
-        out_specs=[vmem] * 2,
-        compiler_params=params,
-        name="unpack",
-    )(back, grad_out)
-    return d_values[None], d_gate[None], d_filter
+        compiler_params=pltpu.CompilerParams(
+            vmem_limit_bytes=56 * 1024 * 1024, collective_id=0, has_side_effects=True
+        ),
+        name="whole",
+    )(skip, grad_out, gate, values, filters, *consts)
+    return d_values.reshape(1, channels, width), d_gate.reshape(1, channels, width), d_filter
 
 
 def solution(mesh):
@@ -230,8 +331,9 @@
         P("ctx", None),
         P("ctx"),
     )
+    grid = (mesh.shape["ctx"] // 8, 4, 2)
     return jax.shard_map(
-        on_device,
+        functools.partial(on_device, grid),
         mesh=mesh,
         in_specs=placed,
         out_specs=(P("rep", None, "ctx"), P("rep", None, "ctx"), P("ctx", None)),

time: 134 us -> 91.2 us (0.68)
  Pallas kernels: 33.1 us -> 85.6 us
  blocking collectives: 46.3 us -> 0 us
  waiting for transfers between devices: 31.4 us -> 0 us
  between operations: 14 us -> 0.65 us
  starting transfers between devices: 6.55 us -> 0 us
  local copies, waits for them, and re-layouts: 1.94 us -> 4.8 us
    pallas_call x3 -> x1, Pallas kernels: 33.1 us -> 85.6 us  [on_device(): pl.pallas_call(functools.partial(whole_kernel, reps, chunks, width, grid)...]
    all_to_all x1 -> x0, blocking collectives: 46.3 us -> none  [on_device(): lax.all_to_all(packed, ('ctx', 'rep'), split_axis=0, concat_axis=0, tiled...]
    all_gather x1 -> x0, waiting for transfers between devices: 30.7 us -> none  [on_device(): d_filter = lax.all_gather(d_filter, 'rep', axis=0, tiled=True)]
    all_to_all x1 -> x0, starting transfers between devices: 6.5 us -> none  [on_device(): lax.all_to_all(results, ('ctx', 'rep'), split_axis=0, concat_axis=0, tile...]
    unnamed x5, local copies, waits for them, and re-layouts: 1.94 us -> 4.8 us
  transfers between devices with their start and end apart: 2 -> 0, of which waited for: 1 -> 0; matrix products, arithmetic and copies ran while one was open for 0% -> 0% of each run, Pallas kernels for 0% -> 0%
where the time goes in v2:
time: 91.2 us; the launch traced here: 91.1 us
  Pallas kernels  85.6 us (94%)
  local copies, waits for them, and re-layouts  4.8 us (5%)
    pallas_call x1, Pallas kernels, on_device(): pl.pallas_call(functools.partial(whole_kernel, reps, chunks, width, grid)...  85.6 us
    unnamed x5, local copies, waits for them, and re-layouts  4.8 us

profile of v2, /device:TPU:1, one launch (start us, length us, event | category | flops | bytes accessed | tf_op | source)
XLA Modules:
  0.0 91.1 jit_solution(10086557170727965799)
XLA Ops:
  0.6 85.6 %whole.1 = (bf16[64,32,128]{2,1,0:T(8,128)(2,1)}, bf16[64,32,128]{2,1,0:T(8,128)(2,1)}, f32[32,8192]{1,0:T(8,128)}) custom-call(f32[32]{0:T(128)} %skip_ref.1, bf16[64,32,128]{2,1,0:T(8,128)(2,1)} %bitcast.7, bf16[64,32,128]{2,1,0:T(8,128)(2,1)} %bitcast.8, bf16[64,32,128]{2,1,0:T(8,128)(2,1)} %bitcast.9, f32[32,8192]{1,0:T(8,128)} %filter_ref.1, ...), custom_call_target="tpu_custom_call" | custom-call | tf_op jit(solution)/shard_map/whole/pallas_call | solution.py:287
  86.3 0.0 copy-start
  86.3 2.0 %copy.19 = bf16[1,2048,128]{2,1,0:T(8,128)(2,1)} copy(bf16[1,2048,128]{2,1,0:T(8,128)(2,1)} %bitcast.6) | data formatting | bytes 1048576
  88.2 1.9 %copy.20 = bf16[1,2048,128]{2,1,0:T(8,128)(2,1)} copy(bf16[1,2048,128]{2,1,0:T(8,128)(2,1)} %bitcast.5) | data formatting | bytes 1048576
  90.1 0.0 copy-done
  90.1 1.0 %copy.21 = f32[32,8192]{1,0:T(8,128)} copy(f32[32,8192]{1,0:T(8,128)S(1)} %copy-done) | data formatting | bytes 2097152
Async XLA Ops:
  86.3 3.8 %copy-start = (f32[32,8192]{1,0:T(8,128)S(1)}, f32[32,8192]{1,0:T(8,128)}, u32[]{:S(2)}) copy-start(f32[32,8192]{1,0:T(8,128)} %get-tuple-element.14) | copy-start | bytes 3145732

commit v3 on v2

--- a/solution.py
+++ b/solution.py
@@ -64,10 +64,14 @@
 
 def whole_kernel(
     reps, chunks, width, grid,
+    skip_hbm, grad_hbm, gate_hbm, value_hbm, filter_hbm,
+    first_hbm, filter_first_hbm, second_hi_hbm, second_lo_hbm, back_hi_hbm, back_lo_hbm, last_hbm, twist_hbm,
+    d_values_hbm, d_gate_hbm, d_filter_hbm,
     skip_ref, grad_ref, gate_ref, value_ref, filter_ref,
     first_ref, filter_first_ref, second_hi_ref, second_lo_ref, back_hi_ref, back_lo_ref, last_ref, twist_ref,
     d_values_ref, d_gate_ref, d_filter_ref,
     send, recv, result_out, back, rows_in, rows_out, filter_rows, filter_spec, cross, spectra, note_out, note_in,
+    in_sem, out_sem,
     send_sem, recv_sem, back_send_sem, back_sem, filter_send_sem, filter_sem, note_send_sem, note_sem,
 ):
     here = 8
@@ -108,6 +112,19 @@
         real, imag = section[:, :width], section[:, width:]
         return jnp.concatenate([real * cos - imag * sin, imag * cos + real * sin], axis=0)
 
+    own = pl.ds(pl.multiple_of(mine, here), here)
+    loads = [
+        pltpu.make_async_copy(src, dst, in_sem.at[n])
+        for n, (src, dst) in enumerate((
+            (grad_hbm, grad_ref), (gate_hbm, gate_ref), (value_hbm, value_ref),
+            (filter_hbm.at[own], filter_ref), (filter_first_hbm, filter_first_ref), (twist_hbm, twist_ref),
+            (second_hi_hbm, second_hi_ref), (second_lo_hbm, second_lo_ref), (first_hbm, first_ref),
+            (back_hi_hbm, back_hi_ref), (back_lo_hbm, back_lo_ref), (last_hbm, last_ref), (skip_hbm, skip_ref),
+        ))
+    ]
+    for load in loads:
+        load.start()
+
     barrier = pltpu.get_barrier_semaphore()
 
     @pl.loop(1, nz * nx)
@@ -117,6 +134,9 @@
     @pl.loop(1, reps * ny)
     def _(step):
         pl.semaphore_signal(barrier, 1, device_id=along_column(step), device_id_type=MESH)
+
+    for load in loads[:3]:
+        load.wait()
 
     @pl.loop(0, chunks)
     def _(j):
@@ -139,21 +159,41 @@
     def _(step):
         note(step).start()
 
-    for n in range(chunks):
-        filter_rows[n * here:(n + 1) * here, :] = filter_ref[pl.ds(mine, here), n * width:(n + 1) * width]
-
-    count = reps * ny - 1
-    pltpu.make_async_copy(note_in.at[pl.ds(0, count)], note_in.at[pl.ds(0, count)], note_sem).wait()
-    pltpu.make_async_copy(note_in.at[pl.ds(0, count)], note_in.at[pl.ds(0, count)], note_send_sem).wait()
-
-    @pl.loop(1, reps * chunks)
-    def _(step):
-        phase = step // chunks
-        i, j = peer(phase), partner(step % chunks)
+    def send_block(phase, i, j):
         pltpu.make_async_remote_copy(
             src_ref=send.at[j, i], dst_ref=recv.at[phase, ctx],
             send_sem=send_sem, recv_sem=recv_sem.at[phase], device_id=(i, j), device_id_type=MESH,
         ).start()
+
+    @pl.loop(1, nz * nx)
+    def _(step):
+        send_block(0, rep, place(z + swing(step // nx, nz), y, x + step % nx))
+
+    @pl.loop(1, reps * ny)
+    def _(step):
+        phase = step // ny
+        send_block(phase, peer(phase), place(z, y + step % ny, x))
+
+    for load in loads[3:]:
+        load.wait()
+
+    for n in range(chunks):
+        filter_rows[n * here:(n + 1) * here, :] = filter_ref[:, n * width:(n + 1) * width]
+
+    count = reps * ny - 1
+    pltpu.make_async_copy(note_in.at[pl.ds(0, count)], note_in.at[pl.ds(0, count)], note_sem).wait()
+    pltpu.make_async_copy(note_in.at[pl.ds(0, count)], note_in.at[pl.ds(0, count)], note_send_sem).wait()
+
+    @pl.loop(1, reps * chunks)
+    def _(step):
+        phase, rest = step // chunks, step % chunks
+        turn_y, turn_x = rest // nz // nx, rest // nz % nx
+        to_row = (phase == 0) & (turn_y == 0)
+        to_column = (rest % nz == 0) & (turn_x == 0)
+
+        @pl.when(jnp.logical_not(to_row | to_column))
+        def _():
+            send_block(phase, peer(phase), partner(rest))
 
     @pl.loop(0, here)
     def _(c):
@@ -218,14 +258,19 @@
                 send_sem=back_send_sem, recv_sem=back_sem.at[phase], device_id=(other, j), device_id_type=MESH,
             ).start()
 
+    def wait_blocks(phase, sem):
+        arrived = recv.at[phase, pl.ds(0, chunks - 1 if phase == 0 else chunks)]
+        pltpu.make_async_copy(arrived, arrived, sem.at[phase]).wait()
+
     for phase in range(reps):
-        blocks = chunks - 1 if phase == 0 else chunks
-        arrived = recv.at[phase, pl.ds(0, blocks)]
-        pltpu.make_async_copy(arrived, arrived, recv_sem.at[phase]).wait()
+        wait_blocks(phase, recv_sem)
+        if phase == reps - 1:
+            for earlier in range(phase):
+                send_back(earlier, 1 if earlier == 0 else 0)
         convolve(phase)
         if phase == 0:
             back[ctx, rep] = result_out[0, ctx]
-        send_back(phase, 1 if phase == 0 else 0)
+    send_back(reps - 1, 0)
 
     factor = scale / math.sqrt(reps * chunks * width)
 
@@ -236,7 +281,6 @@
         parts = dot(last_ref[...], jnp.concatenate([high, low], axis=0))
         filter_rows[pl.ds(c, chunks, stride=here), :] = parts[:chunks] + parts[chunks:]
 
-    own = pl.ds(pl.multiple_of(mine, here), here)
     for n in range(chunks):
         d_filter_ref[own, n * width:(n + 1) * width] = filter_rows[n * here:(n + 1) * here, :]
 
@@ -249,11 +293,12 @@
         ))
         filter_copies[-1].start()
 
+    stores = [pltpu.make_async_copy(d_filter_ref.at[own], d_filter_hbm.at[own], out_sem.at[0])]
+    stores[0].start()
+
     for half in range(reps // 2):
         for phase in (2 * half, 2 * half + 1):
-            blocks = chunks - 1 if phase == 0 else chunks
-            arrived = recv.at[phase, pl.ds(0, blocks)]
-            pltpu.make_async_copy(arrived, arrived, back_sem.at[phase]).wait()
+            wait_blocks(phase, back_sem)
         side = (rep // 2 + half) % 2
         rows = pl.ds(pl.multiple_of(side * 16, 16), 16)
 
@@ -264,8 +309,17 @@
             d_values_ref[k, rows] = block[:, here:].reshape(16, width).astype(BF16)
             d_gate_ref[k, rows] = (grad_ref[k, rows].astype(F32) * mixed).astype(BF16)
 
-    for copy in filter_copies:
+        for src, dst in ((d_values_ref, d_values_hbm), (d_gate_ref, d_gate_hbm)):
+            stores.append(pltpu.make_async_copy(src.at[:, rows], dst.at[:, rows], out_sem.at[len(stores)]))
+            stores[-1].start()
+
+    for phase, copy in enumerate(filter_copies, 1):
         copy.wait()
+        there = pl.ds(pl.multiple_of(peer(phase) * here, here), here)
+        stores.append(pltpu.make_async_copy(d_filter_ref.at[there], d_filter_hbm.at[there], out_sem.at[len(stores)]))
+        stores[-1].start()
+    for store in stores:
+        store.wait()
     sent = send.at[pl.ds(0, chunks - 1)]
     rest = send.at[chunks - 1, pl.ds(0, reps - 1)]
     for sem in (send_sem, back_send_sem):
@@ -273,12 +327,25 @@
         pltpu.make_async_copy(rest, rest, sem).wait()
 
 
+def finish_kernel(parts, *refs):
+    count = (len(refs) - 1) // 2
+    sems = refs[-1]
+    copies = []
+    for n, (src, dst) in enumerate(zip(refs[:count], refs[count:-1])):
+        size = src.shape[0] // parts
+        for part in range(parts):
+            rows = pl.ds(part * size, size)
+            copies.append(pltpu.make_async_copy(src.at[rows], dst.at[rows], sems.at[n, part]))
+            copies[-1].start()
+    for copy in copies:
+        copy.wait()
+
+
 def on_device(grid, grad_out, gate, values, filters, skip):
     reps = lax.axis_size("rep")
     chunks = lax.axis_size("ctx")
     channels, width = values.shape[1:]
-    vmem = pl.BlockSpec(memory_space=pltpu.VMEM)
-    smem = pl.BlockSpec(memory_space=pltpu.SMEM)
+    hbm = pl.BlockSpec(memory_space=pl.ANY)
     grad_out, gate, values = (a.reshape(chunks, channels // chunks, width) for a in (grad_out, gate, values))
     consts = [jnp.asarray(t) for t in tables(chunks, width)]
     rows = chunks * 16
@@ -291,9 +358,18 @@
             jax.ShapeDtypeStruct(values.shape, BF16),
             jax.ShapeDtypeStruct(filters.shape, F32),
         ],
-        in_specs=[smem] + [vmem] * (4 + len(consts)),
-        out_specs=[vmem] * 3,
+        in_specs=[hbm] * (5 + len(consts)),
+        out_specs=[hbm] * 3,
         scratch_shapes=[
+            pltpu.SMEM(skip.shape, F32),
+            pltpu.VMEM(values.shape, BF16),
+            pltpu.VMEM(values.shape, BF16),
+            pltpu.VMEM(values.shape, BF16),
+            pltpu.VMEM((8, filters.shape[1]), F32),
+            *(pltpu.VMEM(c.shape, c.dtype) for c in consts),
+            pltpu.VMEM(values.shape, BF16),
+            pltpu.VMEM(values.shape, BF16),
+            pltpu.VMEM(filters.shape, F32),
             pltpu.VMEM(blocks_back, BF16),
             pltpu.VMEM(blocks, BF16),
             pltpu.VMEM(blocks, BF16),
@@ -306,6 +382,8 @@
             pltpu.VMEM((8, 2 * chunks, 2 * width), F32),
             pltpu.VMEM((8, width), F32),
             pltpu.VMEM((reps * grid[1], 8, width), F32),
+            pltpu.SemaphoreType.DMA((5 + len(consts),)),
+            pltpu.SemaphoreType.DMA((2 * reps,)),
             pltpu.SemaphoreType.DMA,
             pltpu.SemaphoreType.DMA((reps,)),
             pltpu.SemaphoreType.DMA,
@@ -320,6 +398,17 @@
         ),
         name="whole",
     )(skip, grad_out, gate, values, filters, *consts)
+    parts = 4
+    results = (d_values, d_gate, d_filter)
+    d_values, d_gate, d_filter = pl.pallas_call(
+        functools.partial(finish_kernel, parts),
+        out_shape=[jax.ShapeDtypeStruct(a.shape, a.dtype) for a in results],
+        in_specs=[hbm] * 3,
+        out_specs=[hbm] * 3,
+        scratch_shapes=[pltpu.SemaphoreType.DMA((3, parts))],
+        compiler_params=pltpu.CompilerParams(vmem_limit_bytes=56 * 1024 * 1024),
+        name="finish",
+    )(*results)
     return d_values.reshape(1, channels, width), d_gate.reshape(1, channels, width), d_filter
 
 

time: 91.2 us -> 150 us (1.64)
  Pallas kernels: 85.6 us -> 150 us
  local copies, waits for them, and re-layouts: 4.8 us -> 0 us
    pallas_call x0 -> x1, Pallas kernels: none -> 64.7 us  [on_device(): pl.pallas_call(functools.partial(finish_kernel, parts), out_shape=[jax.Sh...]
    unnamed x5 -> x0, local copies, waits for them, and re-layouts: 4.8 us -> none
where the time goes in v3:
time: 150 us
  Pallas kernels  150 us (100%)
    pallas_call x1, Pallas kernels, on_device(): pl.pallas_call(functools.partial(whole_kernel, reps, chunks, width, grid)...  84.9 us
    pallas_call x1, Pallas kernels, on_device(): pl.pallas_call(functools.partial(finish_kernel, parts), out_shape=[jax.Sh...  64.7 us

profile of v3, /device:TPU:1, one launch (start us, length us, event | category | flops | bytes accessed | tf_op | source)
XLA Modules:
  0.0 150.3 jit_solution(3761980489444937050)
XLA Ops:
  0.6 84.9 %whole.1 = (bf16[64,32,128]{2,1,0:T(8,128)(2,1)}, bf16[64,32,128]{2,1,0:T(8,128)(2,1)}, f32[32,8192]{1,0:T(8,128)}) custom-call(f32[32]{0:T(128)} %skip_hbm.1, bf16[64,32,128]{2,1,0:T(8,128)(2,1)} %bitcast.5, bf16[64,32,128]{2,1,0:T(8,128)(2,1)} %bitcast.6, bf16[64,32,128]{2,1,0:T(8,128)(2,1)} %bitcast.7, f32[32,8192]{1,0:T(8,128)} %filter_hbm.1, ...), custom_call_target="tpu_custom_call" | custom-call | tf_op jit(solution)/shard_map/whole/pallas_call | solution.py:354
  85.5 64.7 %finish.1 = (bf16[64,32,128]{2,1,0:T(8,128)(2,1)}, bf16[64,32,128]{2,1,0:T(8,128)(2,1)}, f32[32,8192]{1,0:T(8,128)}) custom-call(bf16[64,32,128]{2,1,0:T(8,128)(2,1)} %get-tuple-element.9.refs_0_, bf16[64,32,128]{2,1,0:T(8,128)(2,1)} %get-tuple-element.10.refs_1_, f32[32,8192]{1,0:T(8,128)} %get-tuple-element.11.refs_2_), custom_call_target="tpu_custom_call" | custom-call | tf_op jit(solution)/shard_map/finish/pallas_call | solution.py:403

commit v4 on v3

--- a/solution.py
+++ b/solution.py
@@ -37,6 +37,8 @@
     second = np.block([[cos, -sin], [sin, cos]])
     second_hi, second_lo = split_np(second)
     back_hi, back_lo = split_np(second.T)
+    second = np.concatenate([second_hi, second_hi, second_lo], axis=0)
+    back = np.concatenate([back_hi, back_hi, back_lo], axis=0)
     last = np.concatenate([np.cos(outer).T, -np.sin(outer).T], axis=1)
     last_hi, last_lo = split_np(last)
     zero = np.zeros_like(last_lo)
@@ -44,7 +46,7 @@
         [np.concatenate([last_hi, last_hi], axis=1), np.concatenate([last_lo, zero], axis=1)], axis=0
     )
     twist = np.stack([np.cos(turn), np.sin(turn)]).astype(np.float32)
-    return fwd_first, filter_first, second_hi, second_lo, back_hi, back_lo, inv_last, twist
+    return fwd_first, filter_first, second, back, inv_last, twist
 
 
 def dot(left, right):
@@ -57,20 +59,20 @@
     return high, low
 
 
-def dot3(left, right_hi, right_lo):
-    high, low = split(left)
-    return dot(high, right_hi) + (dot(low, right_hi) + dot(high, right_lo))
+def split3(array):
+    high, low = split(array)
+    return jnp.concatenate([high, low, high], axis=1)
 
 
 def whole_kernel(
     reps, chunks, width, grid,
     skip_hbm, grad_hbm, gate_hbm, value_hbm, filter_hbm,
-    first_hbm, filter_first_hbm, second_hi_hbm, second_lo_hbm, back_hi_hbm, back_lo_hbm, last_hbm, twist_hbm,
+    first_hbm, filter_first_hbm, second_hbm, back_hbm, last_hbm, twist_hbm,
     d_values_hbm, d_gate_hbm, d_filter_hbm,
     skip_ref, grad_ref, gate_ref, value_ref, filter_ref,
-    first_ref, filter_first_ref, second_hi_ref, second_lo_ref, back_hi_ref, back_lo_ref, last_ref, twist_ref,
+    first_ref, filter_first_ref, second_ref, back_ref, last_ref, twist_ref,
     d_values_ref, d_gate_ref, d_filter_ref,
-    send, recv, result_out, back, rows_in, rows_out, filter_rows, filter_spec, cross, spectra, note_out, note_in,
+    send, recv, result_out, back, rows_in, rows_out, filter_rows, filter_spec, cross, spectra, products, note_out, note_in,
     in_sem, out_sem,
     send_sem, recv_sem, back_send_sem, back_sem, filter_send_sem, filter_sem, note_send_sem, note_sem,
 ):
@@ -118,8 +120,8 @@
         for n, (src, dst) in enumerate((
             (grad_hbm, grad_ref), (gate_hbm, gate_ref), (value_hbm, value_ref),
             (filter_hbm.at[own], filter_ref), (filter_first_hbm, filter_first_ref), (twist_hbm, twist_ref),
-            (second_hi_hbm, second_hi_ref), (second_lo_hbm, second_lo_ref), (first_hbm, first_ref),
-            (back_hi_hbm, back_hi_ref), (back_lo_hbm, back_lo_ref), (last_hbm, last_ref), (skip_hbm, skip_ref),
+            (second_hbm, second_ref), (first_hbm, first_ref),
+            (back_hbm, back_ref), (last_hbm, last_ref), (skip_hbm, skip_ref),
         ))
     ]
     for load in loads:
@@ -146,7 +148,7 @@
         send[j] = both.astype(BF16)
 
     note_out[...] = jnp.zeros_like(note_out)
-    recv[0, ctx] = send[ctx, rep]
+    pltpu.make_async_copy(send.at[ctx, rep], recv.at[0, ctx], recv_sem.at[0]).start()
     pl.semaphore_wait(barrier, nz * nx + reps * ny - 2)
 
     def note(step):
@@ -195,103 +197,106 @@
         def _():
             send_block(phase, peer(phase), partner(rest))
 
-    @pl.loop(0, here)
+    def last_step(both):
+        high, low = split(both)
+        parts = dot(last_ref[...], jnp.concatenate([high, low], axis=0))
+        return parts[:chunks] + parts[chunks:]
+
+    @pl.loop(0, here, unroll=4)
     def _(c):
         high, low = split(filter_rows[pl.ds(c, chunks, stride=here), :])
         section = dot(filter_first_ref[...], jnp.concatenate([high, low, high], axis=0))
-        filter_spec[c] = dot3(twisted(section), second_hi_ref[...], second_lo_ref[...]) * scale
+        filter_spec[c] = dot(split3(twisted(section)), second_ref[...]) * scale
         cross[c] = jnp.zeros((chunks, 2 * width), F32)
 
-    def convolve(phase):
+    def to_spectra(phase):
         rows_in[...] = recv[phase].astype(F32).reshape(chunks * 16, width)
 
-        @pl.loop(0, here)
+        @pl.loop(0, here, unroll=here)
         def _(c):
             value = rows_in[pl.ds(c, chunks, stride=16), :].astype(BF16)
             d_conv = rows_in[pl.ds(c + here, chunks, stride=16), :].astype(BF16)
             pair = jnp.concatenate([value, d_conv], axis=1)
             section = dot(first_ref[...], jnp.concatenate([pair, pair], axis=0))
-            spectra[c] = jnp.concatenate([twisted(section[:, :width]), twisted(section[:, width:])], axis=0)
-
-        flat = spectra[...].reshape(here * 2 * chunks, 2 * width)
-        spectra[...] = dot3(flat, second_hi_ref[...], second_lo_ref[...]).reshape(spectra.shape)
-
-        @pl.loop(0, here)
-        def _(c):
-            vr, vi = spectra[c, :chunks, :width], spectra[c, :chunks, width:]
-            dr, di = spectra[c, chunks:, :width], spectra[c, chunks:, width:]
+            spectra[c, :chunks] = split3(twisted(section[:, :width]))
+            spectra[c, chunks:] = split3(twisted(section[:, width:]))
+
+        full = dot(spectra[...].reshape(here * 2 * chunks, 6 * width), second_ref[...])
+        full = full.reshape(here, 2 * chunks, 2 * width)
+        for c in range(here):
+            vr, vi = full[c, :chunks, :width], full[c, :chunks, width:]
+            dr, di = full[c, chunks:, :width], full[c, chunks:, width:]
             fr, fi = filter_spec[c, :, :width], filter_spec[c, :, width:]
             cross[c, :, :width] += dr * vr + di * vi
             cross[c, :, width:] += di * vr - dr * vi
-            spectra[c, :chunks, :width] = fr * vr - fi * vi
-            spectra[c, :chunks, width:] = fr * vi + fi * vr
-            spectra[c, chunks:, :width] = fr * dr + fi * di
-            spectra[c, chunks:, width:] = fr * di - fi * dr
-
-        flat = spectra[...].reshape(here * 2 * chunks, 2 * width)
-        spectra[...] = dot3(flat, back_hi_ref[...], back_lo_ref[...]).reshape(spectra.shape)
-
-        @pl.loop(0, here)
-        def _(c):
+            products[c, :chunks] = split3(jnp.concatenate([fr * vr - fi * vi, fr * vi + fi * vr], axis=1))
+            products[c, chunks:] = split3(jnp.concatenate([fr * dr + fi * di, fr * di - fi * dr], axis=1))
+
+    def from_products(phase):
+        full = dot(products[...].reshape(here * 2 * chunks, 6 * width), back_ref[...])
+        full = full.reshape(here, 2 * chunks, 2 * width)
+        for c in range(here):
             skip = skip_ref[mine + c]
-            both = jnp.concatenate(
-                [untwisted(spectra[c, :chunks]), untwisted(spectra[c, chunks:])], axis=1
-            )
-            high, low = split(both)
-            parts = dot(last_ref[...], jnp.concatenate([high, low], axis=0))
-            result = parts[:chunks] + parts[chunks:]
+            result = last_step(jnp.concatenate([untwisted(full[c, :chunks]), untwisted(full[c, chunks:])], axis=1))
             value = rows_in[pl.ds(c, chunks, stride=16), :]
             d_conv = rows_in[pl.ds(c + here, chunks, stride=16), :]
             rows_out[pl.ds(c, chunks, stride=16), :] = result[:, :width] + skip * value
             rows_out[pl.ds(c + here, chunks, stride=16), :] = result[:, width:] + skip * d_conv
-
         result_out[phase] = rows_out[...].reshape(chunks, 16, width).astype(BF16)
 
-    def send_back(phase, start):
-        other = peer(phase)
-
-        @pl.loop(start, chunks)
+    def send_back(phase, step):
+        j = partner(step)
+        pltpu.make_async_remote_copy(
+            src_ref=result_out.at[phase, j], dst_ref=back.at[ctx, rep],
+            send_sem=back_send_sem, recv_sem=back_sem.at[phase], device_id=(peer(phase), j), device_id_type=MESH,
+        ).start()
+
+    def wait_blocks(phase, sem):
+        pltpu.make_async_copy(recv.at[phase], recv.at[phase], sem.at[phase]).wait()
+
+    factor = scale / math.sqrt(reps * chunks * width)
+    sibling = (peer(1), ctx)
+
+    def filter_copy(n, phase, device):
+        block = pl.ds(pl.multiple_of(peer(phase) * here, here), here)
+        return pltpu.make_async_remote_copy(
+            src_ref=d_filter_ref.at[block], dst_ref=d_filter_ref.at[block],
+            send_sem=filter_send_sem.at[n], recv_sem=filter_sem.at[n], device_id=device, device_id_type=MESH,
+        )
+
+    to_sibling = filter_copy(0, 0, sibling)
+    across = filter_copy(1, 0, (peer(2), ctx))
+    onward = filter_copy(2, 2, sibling)
+
+    @pl.loop(0, reps)
+    def _(phase):
+        wait_blocks(phase, recv_sem)
+        to_spectra(phase)
+
+        @pl.when(phase == reps - 1)
+        def _():
+            @pl.loop(0, here // 2, unroll=4)
+            def _(g):
+                both = [untwisted(dot(split3(cross[2 * g + e] * factor), back_ref[...])) for e in range(2)]
+                result = last_step(jnp.concatenate(both, axis=1))
+                for e in range(2):
+                    filter_rows[pl.ds(2 * g + e, chunks, stride=here), :] = result[:, e * width:(e + 1) * width]
+
+            for n in range(chunks):
+                d_filter_ref[own, n * width:(n + 1) * width] = filter_rows[n * here:(n + 1) * here, :]
+            across.start()
+            to_sibling.start()
+
+        from_products(phase)
+
+        @pl.when(phase == 0)
+        def _():
+            pltpu.make_async_copy(result_out.at[0, ctx], back.at[ctx, rep], back_sem.at[0]).start()
+
+        @pl.loop(jnp.where(phase == 0, 1, 0), chunks)
         def _(step):
-            j = partner(step)
-            pltpu.make_async_remote_copy(
-                src_ref=result_out.at[phase, j], dst_ref=back.at[ctx, rep],
-                send_sem=back_send_sem, recv_sem=back_sem.at[phase], device_id=(other, j), device_id_type=MESH,
-            ).start()
-
-    def wait_blocks(phase, sem):
-        arrived = recv.at[phase, pl.ds(0, chunks - 1 if phase == 0 else chunks)]
-        pltpu.make_async_copy(arrived, arrived, sem.at[phase]).wait()
-
-    for phase in range(reps):
-        wait_blocks(phase, recv_sem)
-        if phase == reps - 1:
-            for earlier in range(phase):
-                send_back(earlier, 1 if earlier == 0 else 0)
-        convolve(phase)
-        if phase == 0:
-            back[ctx, rep] = result_out[0, ctx]
-    send_back(reps - 1, 0)
-
-    factor = scale / math.sqrt(reps * chunks * width)
-
-    @pl.loop(0, here)
-    def _(c):
-        both = untwisted(dot3(cross[c] * factor, back_hi_ref[...], back_lo_ref[...]))
-        high, low = split(both)
-        parts = dot(last_ref[...], jnp.concatenate([high, low], axis=0))
-        filter_rows[pl.ds(c, chunks, stride=here), :] = parts[:chunks] + parts[chunks:]
-
-    for n in range(chunks):
-        d_filter_ref[own, n * width:(n + 1) * width] = filter_rows[n * here:(n + 1) * here, :]
-
-    filter_copies = []
-    for phase in range(1, reps):
-        filter_copies.append(pltpu.make_async_remote_copy(
-            src_ref=d_filter_ref.at[own], dst_ref=d_filter_ref.at[own],
-            send_sem=filter_send_sem.at[phase], recv_sem=filter_sem.at[phase],
-            device_id=(peer(phase), ctx), device_id_type=MESH,
-        ))
-        filter_copies[-1].start()
+            send_back(phase, step)
+
 
     stores = [pltpu.make_async_copy(d_filter_ref.at[own], d_filter_hbm.at[own], out_sem.at[0])]
     stores[0].start()
@@ -302,7 +307,7 @@
         side = (rep // 2 + half) % 2
         rows = pl.ds(pl.multiple_of(side * 16, 16), 16)
 
-        @pl.loop(0, chunks)
+        @pl.loop(0, chunks, unroll=4)
         def _(k):
             block = back[k, pl.ds(side * 2, 2)].astype(F32)
             mixed = block[:, :here].reshape(16, width)
@@ -312,12 +317,18 @@
         for src, dst in ((d_values_ref, d_values_hbm), (d_gate_ref, d_gate_hbm)):
             stores.append(pltpu.make_async_copy(src.at[:, rows], dst.at[:, rows], out_sem.at[len(stores)]))
             stores[-1].start()
-
-    for phase, copy in enumerate(filter_copies, 1):
-        copy.wait()
+        if half == 0:
+            across.wait_recv()
+            onward.start()
+
+    to_sibling.wait_recv()
+    onward.wait_recv()
+    for phase in range(1, reps):
         there = pl.ds(pl.multiple_of(peer(phase) * here, here), here)
         stores.append(pltpu.make_async_copy(d_filter_ref.at[there], d_filter_hbm.at[there], out_sem.at[len(stores)]))
         stores[-1].start()
+    for copy in (to_sibling, across, onward):
+        copy.wait_send()
     for store in stores:
         store.wait()
     sent = send.at[pl.ds(0, chunks - 1)]
@@ -328,17 +339,25 @@
 
 
 def finish_kernel(parts, *refs):
-    count = (len(refs) - 1) // 2
-    sems = refs[-1]
-    copies = []
-    for n, (src, dst) in enumerate(zip(refs[:count], refs[count:-1])):
-        size = src.shape[0] // parts
-        for part in range(parts):
+    count = (len(refs) - 2) // 3
+    sources, targets, held = refs[:count], refs[count:2 * count], refs[2 * count:3 * count]
+    in_sems, out_sems = refs[-2:]
+    pieces = []
+    for part in range(parts):
+        for n in range(count):
+            size = sources[n].shape[0] // parts
             rows = pl.ds(part * size, size)
-            copies.append(pltpu.make_async_copy(src.at[rows], dst.at[rows], sems.at[n, part]))
-            copies[-1].start()
-    for copy in copies:
-        copy.wait()
+            pieces.append((
+                pltpu.make_async_copy(sources[n].at[rows], held[n].at[rows], in_sems.at[n, part]),
+                pltpu.make_async_copy(held[n].at[rows], targets[n].at[rows], out_sems.at[n, part]),
+            ))
+    for load, _ in pieces:
+        load.start()
+    for load, store in pieces:
+        load.wait()
+        store.start()
+    for _, store in pieces:
+        store.wait()
 
 
 def on_device(grid, grad_out, gate, values, filters, skip):
@@ -379,7 +398,8 @@
             pltpu.VMEM((chunks * 8, width), F32),
             pltpu.VMEM((8, chunks, 2 * width), F32),
             pltpu.VMEM((8, chunks, 2 * width), F32),
-            pltpu.VMEM((8, 2 * chunks, 2 * width), F32),
+            pltpu.VMEM((8, 2 * chunks, 6 * width), BF16),
+            pltpu.VMEM((8, 2 * chunks, 6 * width), BF16),
             pltpu.VMEM((8, width), F32),
             pltpu.VMEM((reps * grid[1], 8, width), F32),
             pltpu.SemaphoreType.DMA((5 + len(consts),)),
@@ -405,7 +425,8 @@
         out_shape=[jax.ShapeDtypeStruct(a.shape, a.dtype) for a in results],
         in_specs=[hbm] * 3,
         out_specs=[hbm] * 3,
-        scratch_shapes=[pltpu.SemaphoreType.DMA((3, parts))],
+        scratch_shapes=[pltpu.VMEM(a.shape, a.dtype) for a in results]
+        + [pltpu.SemaphoreType.DMA((3, parts))] * 2,
         compiler_params=pltpu.CompilerParams(vmem_limit_bytes=56 * 1024 * 1024),
         name="finish",
     )(*results)

time: 150 us -> 69.8 us (0.47)
  Pallas kernels: 150 us -> 69 us
    pallas_call x1, Pallas kernels: 64.7 us -> 2.51 us  [on_device(): pl.pallas_call(functools.partial(finish_kernel, parts), out_shape=[jax.Sh...]
    pallas_call x1, Pallas kernels: 84.9 us -> 66.5 us  [on_device(): pl.pallas_call(functools.partial(whole_kernel, reps, chunks, width, grid)...]
where the time goes in v4:
time: 69.8 us; the launch traced here: 69.6 us
  Pallas kernels  69 us (99%)
    pallas_call x1, Pallas kernels, on_device(): pl.pallas_call(functools.partial(whole_kernel, reps, chunks, width, grid)...  66.5 us
    pallas_call x1, Pallas kernels, on_device(): pl.pallas_call(functools.partial(finish_kernel, parts), out_shape=[jax.Sh...  2.51 us

profile of v4, /device:TPU:1, one launch (start us, length us, event | category | flops | bytes accessed | tf_op | source)
XLA Modules:
  0.0 69.6 jit_solution(1976137414260820132)
XLA Ops:
  0.6 66.5 %whole.1 = (bf16[64,32,128]{2,1,0:T(8,128)(2,1)}, bf16[64,32,128]{2,1,0:T(8,128)(2,1)}, f32[32,8192]{1,0:T(8,128)}) custom-call(f32[32]{0:T(128)} %skip_hbm.1, bf16[64,32,128]{2,1,0:T(8,128)(2,1)} %bitcast.5, bf16[64,32,128]{2,1,0:T(8,128)(2,1)} %bitcast.6, bf16[64,32,128]{2,1,0:T(8,128)(2,1)} %bitcast.7, f32[32,8192]{1,0:T(8,128)} %filter_hbm.1, ...), custom_call_target="tpu_custom_call" | custom-call | tf_op jit(solution)/shard_map/whole/pallas_call | solution.py:373
  67.1 2.5 %finish.1 = (bf16[64,32,128]{2,1,0:T(8,128)(2,1)}, bf16[64,32,128]{2,1,0:T(8,128)(2,1)}, f32[32,8192]{1,0:T(8,128)}) custom-call(bf16[64,32,128]{2,1,0:T(8,128)(2,1)} %get-tuple-element.9.refs_0_, bf16[64,32,128]{2,1,0:T(8,128)(2,1)} %get-tuple-element.10.refs_1_, f32[32,8192]{1,0:T(8,128)} %get-tuple-element.11.refs_2_), custom_call_target="tpu_custom_call" | custom-call | tf_op jit(solution)/shard_map/finish/pallas_call | solution.py:423

commit v5 on v4

--- a/solution.py
+++ b/solution.py
@@ -80,29 +80,41 @@
     nz, ny, nx = grid
     rep = lax.axis_index("rep")
     ctx = lax.axis_index("ctx")
-    z, y, x = ctx // (ny * nx), (ctx // nx) % ny, ctx % nx
+    z, y, x = lax.div(ctx, ny * nx), lax.rem(lax.div(ctx, nx), ny), lax.rem(ctx, nx)
     mine = rep * here
     scale = 1.0 / (chunks * width)
 
-    def place(zz, yy, xx):
-        return (zz % nz) * (ny * nx) + (yy % ny) * nx + xx % nx
-
-    def along_row(step):
-        return rep, place(z + step // nx, y, x + step % nx)
-
-    def along_column(step):
-        return (rep + step // ny) % reps, place(z, y + step % ny, x)
-
-    def swing(step, size):
-        return (step + 1) // 2 * (2 * (step % 2) - 1) + size
-
-    def partner(step):
-        rest = step // nz
-        return place(z + swing(step % nz, nz), y + swing(rest // nx, ny), x + rest % nx)
+    swing_z = [0] + [d * sign for d in range(1, nz // 2) for sign in (1, -1)] + [nz // 2]
+    to_z = [lax.rem(z + step + nz, nz) * (ny * nx) for step in swing_z]
+
+    def to_yx(turn_y, turn_x):
+        return lax.rem(y + turn_y, ny) * nx + lax.rem(x + turn_x, nx)
+
+    stay = to_yx(0, 0)
+
+    def around(start, stop, act):
+        @pl.loop(start, stop)
+        def _(step):
+            phase, rest = lax.div(step, ny * nx), lax.rem(step, ny * nx)
+            turn_x = lax.rem(rest, nx)
+            there = to_yx(lax.div(rest, nx), turn_x)
+            act(phase, turn_x, there)
+
+    def along_row(act):
+        for n, start in enumerate(to_z):
+            for turn_x in range(nx):
+                if n or turn_x:
+                    act(0, start + to_yx(0, turn_x))
+
+    def along_column(act):
+        for phase in range(reps):
+            for turn_y in range(ny):
+                if phase or turn_y:
+                    act(phase, to_z[0] + to_yx(turn_y, 0))
 
     def peer(phase):
-        base = (rep + phase // 2 * 2) % reps
-        return base + phase % 2 * (1 - base % 2 * 2)
+        base = lax.rem(rep + lax.div(phase, 2) * 2, reps)
+        return base + lax.rem(phase, 2) * (1 - lax.rem(base, 2) * 2)
 
     def twisted(section):
         cos, sin = twist_ref[0], twist_ref[1]
@@ -129,18 +141,16 @@
 
     barrier = pltpu.get_barrier_semaphore()
 
-    @pl.loop(1, nz * nx)
-    def _(step):
-        pl.semaphore_signal(barrier, 1, device_id=along_row(step), device_id_type=MESH)
-
-    @pl.loop(1, reps * ny)
-    def _(step):
-        pl.semaphore_signal(barrier, 1, device_id=along_column(step), device_id_type=MESH)
+    def greet(phase, j):
+        pl.semaphore_signal(barrier, 1, device_id=(peer(phase), j), device_id_type=MESH)
+
+    along_row(greet)
+    along_column(greet)
 
     for load in loads[:3]:
         load.wait()
 
-    @pl.loop(0, chunks)
+    @pl.loop(0, chunks, unroll=4)
     def _(j):
         value = value_ref[j].astype(F32)
         d_conv = grad_ref[j].astype(F32) * gate_ref[j].astype(F32)
@@ -151,30 +161,22 @@
     pltpu.make_async_copy(send.at[ctx, rep], recv.at[0, ctx], recv_sem.at[0]).start()
     pl.semaphore_wait(barrier, nz * nx + reps * ny - 2)
 
-    def note(step):
-        return pltpu.make_async_remote_copy(
+    def note(phase, j):
+        pltpu.make_async_remote_copy(
             src_ref=note_out, dst_ref=note_in.at[rep * ny + y],
-            send_sem=note_send_sem, recv_sem=note_sem, device_id=along_column(step), device_id_type=MESH,
-        )
-
-    @pl.loop(1, reps * ny)
-    def _(step):
-        note(step).start()
-
-    def send_block(phase, i, j):
+            send_sem=note_send_sem, recv_sem=note_sem, device_id=(peer(phase), j), device_id_type=MESH,
+        ).start()
+
+    def send_block(phase, j):
+        i = peer(phase)
         pltpu.make_async_remote_copy(
             src_ref=send.at[j, i], dst_ref=recv.at[phase, ctx],
             send_sem=send_sem, recv_sem=recv_sem.at[phase], device_id=(i, j), device_id_type=MESH,
         ).start()
 
-    @pl.loop(1, nz * nx)
-    def _(step):
-        send_block(0, rep, place(z + swing(step // nx, nz), y, x + step % nx))
-
-    @pl.loop(1, reps * ny)
-    def _(step):
-        phase = step // ny
-        send_block(phase, peer(phase), place(z, y + step % ny, x))
+    along_column(note)
+    along_row(send_block)
+    along_column(send_block)
 
     for load in loads[3:]:
         load.wait()
@@ -186,16 +188,15 @@
     pltpu.make_async_copy(note_in.at[pl.ds(0, count)], note_in.at[pl.ds(0, count)], note_sem).wait()
     pltpu.make_async_copy(note_in.at[pl.ds(0, count)], note_in.at[pl.ds(0, count)], note_send_sem).wait()
 
-    @pl.loop(1, reps * chunks)
-    def _(step):
-        phase, rest = step // chunks, step % chunks
-        turn_y, turn_x = rest // nz // nx, rest // nz % nx
-        to_row = (phase == 0) & (turn_y == 0)
-        to_column = (rest % nz == 0) & (turn_x == 0)
-
-        @pl.when(jnp.logical_not(to_row | to_column))
+    def send_ring(phase, turn_x, there):
+        @pl.when(turn_x > 0)
         def _():
-            send_block(phase, peer(phase), partner(rest))
+            send_block(phase, to_z[0] + there)
+
+        for start in to_z[1:]:
+            send_block(phase, start + there)
+
+    around(nx, reps * ny * nx, send_ring)
 
     def last_step(both):
         high, low = split(both)
@@ -244,12 +245,19 @@
             rows_out[pl.ds(c + here, chunks, stride=16), :] = result[:, width:] + skip * d_conv
         result_out[phase] = rows_out[...].reshape(chunks, 16, width).astype(BF16)
 
-    def send_back(phase, step):
-        j = partner(step)
+    def send_back(phase, j):
         pltpu.make_async_remote_copy(
             src_ref=result_out.at[phase, j], dst_ref=back.at[ctx, rep],
             send_sem=back_send_sem, recv_sem=back_sem.at[phase], device_id=(peer(phase), j), device_id_type=MESH,
         ).start()
+
+    def send_back_ring(phase, turn_x, there):
+        @pl.when((phase > 0) | (there != stay))
+        def _():
+            send_back(phase, to_z[0] + there)
+
+        for start in to_z[1:]:
+            send_back(phase, start + there)
 
     def wait_blocks(phase, sem):
         pltpu.make_async_copy(recv.at[phase], recv.at[phase], sem.at[phase]).wait()
@@ -293,10 +301,7 @@
         def _():
             pltpu.make_async_copy(result_out.at[0, ctx], back.at[ctx, rep], back_sem.at[0]).start()
 
-        @pl.loop(jnp.where(phase == 0, 1, 0), chunks)
-        def _(step):
-            send_back(phase, step)
-
+        around(phase * (ny * nx), (phase + 1) * (ny * nx), send_back_ring)
 
     stores = [pltpu.make_async_copy(d_filter_ref.at[own], d_filter_hbm.at[own], out_sem.at[0])]
     stores[0].start()

time: 69.8 us -> 67.6 us (0.968)
  Pallas kernels: 69 us -> 66.8 us
    pallas_call x1, Pallas kernels: 66.5 us -> 64.3 us  [on_device(): pl.pallas_call(functools.partial(whole_kernel, reps, chunks, width, grid)...]
where the time goes in v5:
time: 67.6 us; the launch traced here: 67.5 us
  Pallas kernels  66.8 us (99%)
    pallas_call x1, Pallas kernels, on_device(): pl.pallas_call(functools.partial(whole_kernel, reps, chunks, width, grid)...  64.3 us
    pallas_call x1, Pallas kernels, on_device(): pl.pallas_call(functools.partial(finish_kernel, parts), out_shape=[jax.Sh...  2.51 us

profile of v5, /device:TPU:1, one launch (start us, length us, event | category | flops | bytes accessed | tf_op | source)
XLA Modules:
  0.0 67.5 jit_solution(315313438329703655)
XLA Ops:
  0.6 64.3 %whole.1 = (bf16[64,32,128]{2,1,0:T(8,128)(2,1)}, bf16[64,32,128]{2,1,0:T(8,128)(2,1)}, f32[32,8192]{1,0:T(8,128)}) custom-call(f32[32]{0:T(128)} %skip_hbm.1, bf16[64,32,128]{2,1,0:T(8,128)(2,1)} %bitcast.5, bf16[64,32,128]{2,1,0:T(8,128)(2,1)} %bitcast.6, bf16[64,32,128]{2,1,0:T(8,128)(2,1)} %bitcast.7, f32[32,8192]{1,0:T(8,128)} %filter_hbm.1, ...), custom_call_target="tpu_custom_call" | custom-call | tf_op jit(solution)/shard_map/whole/pallas_call | solution.py:378
  65.0 2.5 %finish.1 = (bf16[64,32,128]{2,1,0:T(8,128)(2,1)}, bf16[64,32,128]{2,1,0:T(8,128)(2,1)}, f32[32,8192]{1,0:T(8,128)}) custom-call(bf16[64,32,128]{2,1,0:T(8,128)(2,1)} %get-tuple-element.9.refs_0_, bf16[64,32,128]{2,1,0:T(8,128)(2,1)} %get-tuple-element.10.refs_1_, f32[32,8192]{1,0:T(8,128)} %get-tuple-element.11.refs_2_), custom_call_target="tpu_custom_call" | custom-call | tf_op jit(solution)/shard_map/finish/pallas_call | solution.py:428

commit v6 on v5

--- a/solution.py
+++ b/solution.py
@@ -68,12 +68,12 @@
     reps, chunks, width, grid,
     skip_hbm, grad_hbm, gate_hbm, value_hbm, filter_hbm,
     first_hbm, filter_first_hbm, second_hbm, back_hbm, last_hbm, twist_hbm,
-    d_values_hbm, d_gate_hbm, d_filter_hbm,
+    back, d_filter_hbm,
     skip_ref, grad_ref, gate_ref, value_ref, filter_ref,
     first_ref, filter_first_ref, second_ref, back_ref, last_ref, twist_ref,
-    d_values_ref, d_gate_ref, d_filter_ref,
-    send, recv, result_out, back, rows_in, rows_out, filter_rows, filter_spec, cross, spectra, products, note_out, note_in,
-    in_sem, out_sem,
+    d_filter_ref,
+    send, recv, result_out, rows_in, rows_out, filter_rows, filter_spec, cross, spectra, products, note_out, note_in,
+    in_sem, own_sem,
     send_sem, recv_sem, back_send_sem, back_sem, filter_send_sem, filter_sem, note_send_sem, note_sem,
 ):
     here = 8
@@ -164,7 +164,8 @@
     def note(phase, j):
         pltpu.make_async_remote_copy(
             src_ref=note_out, dst_ref=note_in.at[rep * ny + y],
-            send_sem=note_send_sem, recv_sem=note_sem, device_id=(peer(phase), j), device_id_type=MESH,
+            send_sem=note_send_sem, recv_sem=note_sem.at[rep * ny + y],
+            device_id=(peer(phase), j), device_id_type=MESH,
         ).start()
 
     def send_block(phase, j):
@@ -184,19 +185,15 @@
     for n in range(chunks):
         filter_rows[n * here:(n + 1) * here, :] = filter_ref[:, n * width:(n + 1) * width]
 
-    count = reps * ny - 1
-    pltpu.make_async_copy(note_in.at[pl.ds(0, count)], note_in.at[pl.ds(0, count)], note_sem).wait()
-    pltpu.make_async_copy(note_in.at[pl.ds(0, count)], note_in.at[pl.ds(0, count)], note_send_sem).wait()
-
-    def send_ring(phase, turn_x, there):
-        @pl.when(turn_x > 0)
-        def _():
-            send_block(phase, to_z[0] + there)
-
-        for start in to_z[1:]:
-            send_block(phase, start + there)
-
-    around(nx, reps * ny * nx, send_ring)
+    @pl.loop(1, reps * ny)
+    def _(step):
+        there = lax.rem(step, ny)
+        sender = peer(lax.div(step, ny)) * ny + lax.rem(y + there, ny)
+        pltpu.make_async_copy(note_in.at[sender], note_in.at[sender], note_sem.at[sender]).wait()
+        for turn_x in range(nx):
+            for start in to_z[0 if turn_x else 1:]:
+                send_block(lax.div(step, ny), start + to_yx(there, turn_x))
+
 
     def last_step(both):
         high, low = split(both)
@@ -265,16 +262,17 @@
     factor = scale / math.sqrt(reps * chunks * width)
     sibling = (peer(1), ctx)
 
-    def filter_copy(n, phase, device):
+    def filter_copy(n, src, phase, device):
         block = pl.ds(pl.multiple_of(peer(phase) * here, here), here)
         return pltpu.make_async_remote_copy(
-            src_ref=d_filter_ref.at[block], dst_ref=d_filter_ref.at[block],
+            src_ref=src if phase == 0 else src.at[block], dst_ref=d_filter_hbm.at[block],
             send_sem=filter_send_sem.at[n], recv_sem=filter_sem.at[n], device_id=device, device_id_type=MESH,
         )
 
-    to_sibling = filter_copy(0, 0, sibling)
-    across = filter_copy(1, 0, (peer(2), ctx))
-    onward = filter_copy(2, 2, sibling)
+    to_sibling = filter_copy(0, d_filter_ref, 0, sibling)
+    across = filter_copy(1, d_filter_ref, 0, (peer(2), ctx))
+    onward = filter_copy(2, d_filter_hbm, 2, sibling)
+    own_store = pltpu.make_async_copy(d_filter_ref, d_filter_hbm.at[own], own_sem)
 
     @pl.loop(0, reps)
     def _(phase):
@@ -291,9 +289,10 @@
                     filter_rows[pl.ds(2 * g + e, chunks, stride=here), :] = result[:, e * width:(e + 1) * width]
 
             for n in range(chunks):
-                d_filter_ref[own, n * width:(n + 1) * width] = filter_rows[n * here:(n + 1) * here, :]
+                d_filter_ref[:, n * width:(n + 1) * width] = filter_rows[n * here:(n + 1) * here, :]
             across.start()
             to_sibling.start()
+            own_store.start()
 
         from_products(phase)
 
@@ -303,39 +302,19 @@
 
         around(phase * (ny * nx), (phase + 1) * (ny * nx), send_back_ring)
 
-    stores = [pltpu.make_async_copy(d_filter_ref.at[own], d_filter_hbm.at[own], out_sem.at[0])]
-    stores[0].start()
-
-    for half in range(reps // 2):
-        for phase in (2 * half, 2 * half + 1):
-            wait_blocks(phase, back_sem)
-        side = (rep // 2 + half) % 2
-        rows = pl.ds(pl.multiple_of(side * 16, 16), 16)
-
-        @pl.loop(0, chunks, unroll=4)
-        def _(k):
-            block = back[k, pl.ds(side * 2, 2)].astype(F32)
-            mixed = block[:, :here].reshape(16, width)
-            d_values_ref[k, rows] = block[:, here:].reshape(16, width).astype(BF16)
-            d_gate_ref[k, rows] = (grad_ref[k, rows].astype(F32) * mixed).astype(BF16)
-
-        for src, dst in ((d_values_ref, d_values_hbm), (d_gate_ref, d_gate_hbm)):
-            stores.append(pltpu.make_async_copy(src.at[:, rows], dst.at[:, rows], out_sem.at[len(stores)]))
-            stores[-1].start()
-        if half == 0:
-            across.wait_recv()
-            onward.start()
-
+    for phase in range(reps // 2):
+        wait_blocks(phase, back_sem)
+    across.wait_recv()
+    onward.start()
+    for phase in range(reps // 2, reps):
+        wait_blocks(phase, back_sem)
     to_sibling.wait_recv()
     onward.wait_recv()
-    for phase in range(1, reps):
-        there = pl.ds(pl.multiple_of(peer(phase) * here, here), here)
-        stores.append(pltpu.make_async_copy(d_filter_ref.at[there], d_filter_hbm.at[there], out_sem.at[len(stores)]))
-        stores[-1].start()
+    own_store.wait()
     for copy in (to_sibling, across, onward):
         copy.wait_send()
-    for store in stores:
-        store.wait()
+    notes = note_in.at[pl.ds(0, reps * ny - 1)]
+    pltpu.make_async_copy(notes, notes, note_send_sem).wait()
     sent = send.at[pl.ds(0, chunks - 1)]
     rest = send.at[chunks - 1, pl.ds(0, reps - 1)]
     for sem in (send_sem, back_send_sem):
@@ -343,26 +322,46 @@
         pltpu.make_async_copy(rest, rest, sem).wait()
 
 
-def finish_kernel(parts, *refs):
-    count = (len(refs) - 2) // 3
-    sources, targets, held = refs[:count], refs[count:2 * count], refs[2 * count:3 * count]
-    in_sems, out_sems = refs[-2:]
-    pieces = []
+def finish_kernel(
+    parts, back_hbm, grad_hbm, filter_hbm, d_values_hbm, d_gate_hbm, d_filter_hbm,
+    back, grad, kept, d_values, d_gate, in_sem, out_sem,
+):
+    chunks, reps, rows, width = back.shape
+    here = rows // 2
+    size, kept_size = chunks // parts, kept.shape[0] // parts
+    loads, stores = [], []
     for part in range(parts):
-        for n in range(count):
-            size = sources[n].shape[0] // parts
-            rows = pl.ds(part * size, size)
-            pieces.append((
-                pltpu.make_async_copy(sources[n].at[rows], held[n].at[rows], in_sems.at[n, part]),
-                pltpu.make_async_copy(held[n].at[rows], targets[n].at[rows], out_sems.at[n, part]),
+        cut, kept_cut = pl.ds(part * size, size), pl.ds(part * kept_size, kept_size)
+        loads.append([
+            pltpu.make_async_copy(src.at[c], dst.at[c], in_sem.at[n, part])
+            for n, (src, dst, c) in enumerate(((back_hbm, back, cut), (grad_hbm, grad, cut), (filter_hbm, kept, kept_cut)))
+        ])
+        stores.append([
+            pltpu.make_async_copy(src.at[c], dst.at[c], out_sem.at[n, part])
+            for n, (src, dst, c) in enumerate((
+                (d_values, d_values_hbm, cut), (d_gate, d_gate_hbm, cut), (kept, d_filter_hbm, kept_cut)
             ))
-    for load, _ in pieces:
-        load.start()
-    for load, store in pieces:
-        load.wait()
-        store.start()
-    for _, store in pieces:
-        store.wait()
+        ])
+        for load in loads[-1]:
+            load.start()
+    for part in range(parts):
+        loads[part][0].wait()
+        loads[part][1].wait()
+
+        @pl.loop(part * size, (part + 1) * size, unroll=4)
+        def _(k):
+            block = back[k].astype(F32)
+            mixed = block[:, :here].reshape(reps * here, width)
+            d_values[k] = block[:, here:].reshape(reps * here, width).astype(BF16)
+            d_gate[k] = (grad[k].astype(F32) * mixed).astype(BF16)
+
+        stores[part][0].start()
+        stores[part][1].start()
+        loads[part][2].wait()
+        stores[part][2].start()
+    for group in stores:
+        for store in group:
+            store.wait()
 
 
 def on_device(grid, grad_out, gate, values, filters, skip):
@@ -375,15 +374,14 @@
     rows = chunks * 16
     blocks = (reps, chunks, 16, width)
     blocks_back = (chunks, reps, 16, width)
-    d_values, d_gate, d_filter = pl.pallas_call(
+    back, d_filter = pl.pallas_call(
         functools.partial(whole_kernel, reps, chunks, width, grid),
         out_shape=[
-            jax.ShapeDtypeStruct(values.shape, BF16),
-            jax.ShapeDtypeStruct(values.shape, BF16),
+            jax.ShapeDtypeStruct(blocks_back, BF16),
             jax.ShapeDtypeStruct(filters.shape, F32),
         ],
         in_specs=[hbm] * (5 + len(consts)),
-        out_specs=[hbm] * 3,
+        out_specs=[hbm] * 2,
         scratch_shapes=[
             pltpu.SMEM(skip.shape, F32),
             pltpu.VMEM(values.shape, BF16),
@@ -391,13 +389,10 @@
             pltpu.VMEM(values.shape, BF16),
             pltpu.VMEM((8, filters.shape[1]), F32),
             *(pltpu.VMEM(c.shape, c.dtype) for c in consts),
-            pltpu.VMEM(values.shape, BF16),
-            pltpu.VMEM(values.shape, BF16),
-            pltpu.VMEM(filters.shape, F32),
+            pltpu.VMEM((8, filters.shape[1]), F32),
             pltpu.VMEM(blocks_back, BF16),
             pltpu.VMEM(blocks, BF16),
             pltpu.VMEM(blocks, BF16),
-            pltpu.VMEM(blocks_back, BF16),
             pltpu.VMEM((rows, width), F32),
             pltpu.VMEM((rows, width), F32),
             pltpu.VMEM((chunks * 8, width), F32),
@@ -408,7 +403,7 @@
             pltpu.VMEM((8, width), F32),
             pltpu.VMEM((reps * grid[1], 8, width), F32),
             pltpu.SemaphoreType.DMA((5 + len(consts),)),
-            pltpu.SemaphoreType.DMA((2 * reps,)),
+            pltpu.SemaphoreType.DMA,
             pltpu.SemaphoreType.DMA,
             pltpu.SemaphoreType.DMA((reps,)),
             pltpu.SemaphoreType.DMA,
@@ -416,7 +411,7 @@
             pltpu.SemaphoreType.DMA((reps,)),
             pltpu.SemaphoreType.DMA((reps,)),
             pltpu.SemaphoreType.DMA,
-            pltpu.SemaphoreType.DMA,
+            pltpu.SemaphoreType.DMA((reps * grid[1],)),
         ],
         compiler_params=pltpu.CompilerParams(
             vmem_limit_bytes=56 * 1024 * 1024, collective_id=0, has_side_effects=True
@@ -424,17 +419,27 @@
         name="whole",
     )(skip, grad_out, gate, values, filters, *consts)
     parts = 4
-    results = (d_values, d_gate, d_filter)
     d_values, d_gate, d_filter = pl.pallas_call(
         functools.partial(finish_kernel, parts),
-        out_shape=[jax.ShapeDtypeStruct(a.shape, a.dtype) for a in results],
+        out_shape=[
+            jax.ShapeDtypeStruct(values.shape, BF16),
+            jax.ShapeDtypeStruct(values.shape, BF16),
+            jax.ShapeDtypeStruct(filters.shape, F32),
+        ],
         in_specs=[hbm] * 3,
         out_specs=[hbm] * 3,
-        scratch_shapes=[pltpu.VMEM(a.shape, a.dtype) for a in results]
-        + [pltpu.SemaphoreType.DMA((3, parts))] * 2,
+        scratch_shapes=[
+            pltpu.VMEM(blocks_back, BF16),
+            pltpu.VMEM(values.shape, BF16),
+            pltpu.VMEM(filters.shape, F32),
+            pltpu.VMEM(values.shape, BF16),
+            pltpu.VMEM(values.shape, BF16),
+            pltpu.SemaphoreType.DMA((3, parts)),
+            pltpu.SemaphoreType.DMA((3, parts)),
+        ],
         compiler_params=pltpu.CompilerParams(vmem_limit_bytes=56 * 1024 * 1024),
         name="finish",
-    )(*results)
+    )(back, grad_out, d_filter)
     return d_values.reshape(1, channels, width), d_gate.reshape(1, channels, width), d_filter
 
 

time: 67.6 us -> 65.3 us (0.966)
  Pallas kernels: 66.8 us -> 64.5 us
    pallas_call x1, Pallas kernels: 64.3 us -> 61.8 us  [on_device(): pl.pallas_call(functools.partial(whole_kernel, reps, chunks, width, grid)...]
where the time goes in v6:
time: 65.3 us; the launch traced here: 65.1 us
  Pallas kernels  64.5 us (99%)
    pallas_call x1, Pallas kernels, on_device(): pl.pallas_call(functools.partial(whole_kernel, reps, chunks, width, grid)...  61.8 us
    pallas_call x1, Pallas kernels, on_device(): pl.pallas_call(functools.partial(finish_kernel, parts), out_shape=[jax.Sh...  2.65 us

profile of v6, /device:TPU:1, one launch (start us, length us, event | category | flops | bytes accessed | tf_op | source)
XLA Modules:
  0.0 65.1 jit_solution(8040779795438538837)
XLA Ops:
  0.6 61.8 %whole.1 = (bf16[64,4,16,128]{3,2,1,0:T(8,128)(2,1)}, f32[32,8192]{1,0:T(8,128)}) custom-call(f32[32]{0:T(128)} %skip_hbm.1, bf16[64,32,128]{2,1,0:T(8,128)(2,1)} %bitcast.5, bf16[64,32,128]{2,1,0:T(8,128)(2,1)} %bitcast.7, bf16[64,32,128]{2,1,0:T(8,128)(2,1)} %bitcast.8, f32[32,8192]{1,0:T(8,128)} %filter_hbm.1, bf16[128,128]{1,0:T(8,128)(2,1)} %constant.12.clone.first_hbm, ...), custom_call_target="tpu_custom_call" | custom-call | tf_op jit(solution)/shard_map/whole/pallas_call | solution.py:377
  62.5 2.6 %finish.1 = (bf16[64,32,128]{2,1,0:T(8,128)(2,1)}, bf16[64,32,128]{2,1,0:T(8,128)(2,1)}, f32[32,8192]{1,0:T(8,128)}) custom-call(bf16[64,4,16,128]{3,2,1,0:T(8,128)(2,1)} %get-tuple-element.8.back_hbm, bf16[64,32,128]{2,1,0:T(8,128)(2,1)} %bitcast.6, f32[32,8192]{1,0:T(8,128)} %get-tuple-element.9.filter_hbm), custom_call_target="tpu_custom_call" | custom-call | tf_op jit(solution)/shard_map/finish/pallas_call | solution.py:422

commit v7 on v6

--- a/solution.py
+++ b/solution.py
@@ -100,6 +100,21 @@
             there = to_yx(lax.div(rest, nx), turn_x)
             act(phase, turn_x, there)
 
+    tiers = ((0, 1), (1, nz))
+
+    def early_first(act):
+        for low, high in tiers:
+            @pl.loop(0, ny * nx)
+            def _(rest):
+                there = to_yx(lax.div(rest, nx), lax.rem(rest, nx))
+                if high == low + 1:
+                    act(low * (ny * nx) + there)
+                else:
+                    for start in to_z:
+                        @pl.when((start >= low * (ny * nx)) & (start < high * (ny * nx)))
+                        def _():
+                            act(start + there)
+
     def along_row(act):
         for n, start in enumerate(to_z):
             for turn_x in range(nx):
@@ -179,12 +194,6 @@
     along_row(send_block)
     along_column(send_block)
 
-    for load in loads[3:]:
-        load.wait()
-
-    for n in range(chunks):
-        filter_rows[n * here:(n + 1) * here, :] = filter_ref[:, n * width:(n + 1) * width]
-
     @pl.loop(1, reps * ny)
     def _(step):
         there = lax.rem(step, ny)
@@ -194,6 +203,12 @@
             for start in to_z[0 if turn_x else 1:]:
                 send_block(lax.div(step, ny), start + to_yx(there, turn_x))
 
+
+    for load in loads[3:]:
+        load.wait()
+
+    for n in range(chunks):
+        filter_rows[n * here:(n + 1) * here, :] = filter_ref[:, n * width:(n + 1) * width]
 
     def last_step(both):
         high, low = split(both)
@@ -300,7 +315,13 @@
         def _():
             pltpu.make_async_copy(result_out.at[0, ctx], back.at[ctx, rep], back_sem.at[0]).start()
 
-        around(phase * (ny * nx), (phase + 1) * (ny * nx), send_back_ring)
+        @pl.when(phase < reps - 1)
+        def _():
+            around(phase * (ny * nx), (phase + 1) * (ny * nx), send_back_ring)
+
+        @pl.when(phase == reps - 1)
+        def _():
+            early_first(lambda j: send_back(reps - 1, j))
 
     for phase in range(reps // 2):
         wait_blocks(phase, back_sem)

time: 65.3 us -> 63.4 us (0.971)
  Pallas kernels: 64.5 us -> 62.6 us
    pallas_call x1, Pallas kernels: 61.8 us -> 60 us  [on_device(): pl.pallas_call(functools.partial(whole_kernel, reps, chunks, width, grid)...]
where the time goes in v7:
time: 63.4 us; the launch traced here: 63.2 us
  Pallas kernels  62.6 us (99%)
  between operations  0.64 us (1%)
    pallas_call x1, Pallas kernels, on_device(): pl.pallas_call(functools.partial(whole_kernel, reps, chunks, width, grid)...  60 us
    pallas_call x1, Pallas kernels, on_device(): pl.pallas_call(functools.partial(finish_kernel, parts), out_shape=[jax.Sh...  2.65 us

profile of v7, /device:TPU:1, one launch (start us, length us, event | category | flops | bytes accessed | tf_op | source)
XLA Modules:
  0.0 63.2 jit_solution(13078817833289143976)
XLA Ops:
  0.6 60.0 %whole.1 = (bf16[64,4,16,128]{3,2,1,0:T(8,128)(2,1)}, f32[32,8192]{1,0:T(8,128)}) custom-call(f32[32]{0:T(128)} %skip_hbm.1, bf16[64,32,128]{2,1,0:T(8,128)(2,1)} %bitcast.5, bf16[64,32,128]{2,1,0:T(8,128)(2,1)} %bitcast.7, bf16[64,32,128]{2,1,0:T(8,128)(2,1)} %bitcast.8, f32[32,8192]{1,0:T(8,128)} %filter_hbm.1, bf16[128,128]{1,0:T(8,128)(2,1)} %constant.12.clone.first_hbm, ...), custom_call_target="tpu_custom_call" | custom-call | tf_op jit(solution)/shard_map/whole/pallas_call | solution.py:398
  60.6 2.6 %finish.1 = (bf16[64,32,128]{2,1,0:T(8,128)(2,1)}, bf16[64,32,128]{2,1,0:T(8,128)(2,1)}, f32[32,8192]{1,0:T(8,128)}) custom-call(bf16[64,4,16,128]{3,2,1,0:T(8,128)(2,1)} %get-tuple-element.8.back_hbm, bf16[64,32,128]{2,1,0:T(8,128)(2,1)} %bitcast.6, f32[32,8192]{1,0:T(8,128)} %get-tuple-element.9.filter_hbm), custom_call_target="tpu_custom_call" | custom-call | tf_op jit(solution)/shard_map/finish/pallas_call | solution.py:443

commit v8 on v7

--- a/solution.py
+++ b/solution.py
@@ -223,7 +223,7 @@
         cross[c] = jnp.zeros((chunks, 2 * width), F32)
 
     def to_spectra(phase):
-        rows_in[...] = recv[phase].astype(F32).reshape(chunks * 16, width)
+        rows_in[:chunks * 16] = recv[phase].astype(F32).reshape(chunks * 16, width)
 
         @pl.loop(0, here, unroll=here)
         def _(c):
@@ -255,7 +255,7 @@
             d_conv = rows_in[pl.ds(c + here, chunks, stride=16), :]
             rows_out[pl.ds(c, chunks, stride=16), :] = result[:, :width] + skip * value
             rows_out[pl.ds(c + here, chunks, stride=16), :] = result[:, width:] + skip * d_conv
-        result_out[phase] = rows_out[...].reshape(chunks, 16, width).astype(BF16)
+        result_out[phase] = rows_out[:chunks * 16].reshape(chunks, 16, width).astype(BF16)
 
     def send_back(phase, j):
         pltpu.make_async_remote_copy(
@@ -414,9 +414,9 @@
             pltpu.VMEM(blocks_back, BF16),
             pltpu.VMEM(blocks, BF16),
             pltpu.VMEM(blocks, BF16),
-            pltpu.VMEM((rows, width), F32),
-            pltpu.VMEM((rows, width), F32),
-            pltpu.VMEM((chunks * 8, width), F32),
+            pltpu.VMEM((rows + 16, width), F32),
+            pltpu.VMEM((rows + 16, width), F32),
+            pltpu.VMEM((chunks * 8 + 8, width), F32),
             pltpu.VMEM((8, chunks, 2 * width), F32),
             pltpu.VMEM((8, chunks, 2 * width), F32),
             pltpu.VMEM((8, 2 * chunks, 6 * width), BF16),

time: 63.4 us -> 63.4 us (level)
  no operation moved by 1% of the time
where the time goes in v8:
time: 63.4 us; the launch traced here: 63.2 us
  Pallas kernels  62.6 us (99%)
  between operations  0.64 us (1%)
    pallas_call x1, Pallas kernels, on_device(): pl.pallas_call(functools.partial(whole_kernel, reps, chunks, width, grid)...  60 us
    pallas_call x1, Pallas kernels, on_device(): pl.pallas_call(functools.partial(finish_kernel, parts), out_shape=[jax.Sh...  2.65 us

profile of v8, /device:TPU:1, one launch (start us, length us, event | category | flops | bytes accessed | tf_op | source)
XLA Modules:
  0.0 63.2 jit_solution(6200696620376899272)
XLA Ops:
  0.6 60.0 %whole.1 = (bf16[64,4,16,128]{3,2,1,0:T(8,128)(2,1)}, f32[32,8192]{1,0:T(8,128)}) custom-call(f32[32]{0:T(128)} %skip_hbm.1, bf16[64,32,128]{2,1,0:T(8,128)(2,1)} %bitcast.5, bf16[64,32,128]{2,1,0:T(8,128)(2,1)} %bitcast.7, bf16[64,32,128]{2,1,0:T(8,128)(2,1)} %bitcast.8, f32[32,8192]{1,0:T(8,128)} %filter_hbm.1, bf16[128,128]{1,0:T(8,128)(2,1)} %constant.12.clone.first_hbm, ...), custom_call_target="tpu_custom_call" | custom-call | tf_op jit(solution)/shard_map/whole/pallas_call | solution.py:398
  60.6 2.6 %finish.1 = (bf16[64,32,128]{2,1,0:T(8,128)(2,1)}, bf16[64,32,128]{2,1,0:T(8,128)(2,1)}, f32[32,8192]{1,0:T(8,128)}) custom-call(bf16[64,4,16,128]{3,2,1,0:T(8,128)(2,1)} %get-tuple-element.8.back_hbm, bf16[64,32,128]{2,1,0:T(8,128)(2,1)} %bitcast.6, f32[32,8192]{1,0:T(8,128)} %get-tuple-element.9.filter_hbm), custom_call_target="tpu_custom_call" | custom-call | tf_op jit(solution)/shard_map/finish/pallas_call | solution.py:443

commit v9 on v8

--- a/solution.py
+++ b/solution.py
@@ -90,16 +90,6 @@
     def to_yx(turn_y, turn_x):
         return lax.rem(y + turn_y, ny) * nx + lax.rem(x + turn_x, nx)
 
-    stay = to_yx(0, 0)
-
-    def around(start, stop, act):
-        @pl.loop(start, stop)
-        def _(step):
-            phase, rest = lax.div(step, ny * nx), lax.rem(step, ny * nx)
-            turn_x = lax.rem(rest, nx)
-            there = to_yx(lax.div(rest, nx), turn_x)
-            act(phase, turn_x, there)
-
     tiers = ((0, 1), (1, nz))
 
     def early_first(act):
@@ -263,14 +253,6 @@
             send_sem=back_send_sem, recv_sem=back_sem.at[phase], device_id=(peer(phase), j), device_id_type=MESH,
         ).start()
 
-    def send_back_ring(phase, turn_x, there):
-        @pl.when((phase > 0) | (there != stay))
-        def _():
-            send_back(phase, to_z[0] + there)
-
-        for start in to_z[1:]:
-            send_back(phase, start + there)
-
     def wait_blocks(phase, sem):
         pltpu.make_async_copy(recv.at[phase], recv.at[phase], sem.at[phase]).wait()
 
@@ -315,13 +297,12 @@
         def _():
             pltpu.make_async_copy(result_out.at[0, ctx], back.at[ctx, rep], back_sem.at[0]).start()
 
-        @pl.when(phase < reps - 1)
-        def _():
-            around(phase * (ny * nx), (phase + 1) * (ny * nx), send_back_ring)
-
-        @pl.when(phase == reps - 1)
-        def _():
-            early_first(lambda j: send_back(reps - 1, j))
+        def send_result(j):
+            @pl.when((phase > 0) | (j != ctx))
+            def _():
+                send_back(phase, j)
+
+        early_first(send_result)
 
     for phase in range(reps // 2):
         wait_blocks(phase, back_sem)

time: 63.4 us -> 63.4 us (level)
  no operation moved by 1% of the time
where the time goes in v9:
time: 63.4 us; the launch traced here: 63.2 us
  Pallas kernels  62.6 us (99%)
  between operations  0.64 us (1%)
    pallas_call x1, Pallas kernels, on_device(): pl.pallas_call(functools.partial(whole_kernel, reps, chunks, width, grid)...  60 us
    pallas_call x1, Pallas kernels, on_device(): pl.pallas_call(functools.partial(finish_kernel, parts), out_shape=[jax.Sh...  2.65 us

profile of v9, /device:TPU:1, one launch (start us, length us, event | category | flops | bytes accessed | tf_op | source)
XLA Modules:
  0.0 63.2 jit_solution(13829437912430924291)
XLA Ops:
  0.6 60.0 %whole.1 = (bf16[64,4,16,128]{3,2,1,0:T(8,128)(2,1)}, f32[32,8192]{1,0:T(8,128)}) custom-call(f32[32]{0:T(128)} %skip_hbm.1, bf16[64,32,128]{2,1,0:T(8,128)(2,1)} %bitcast.5, bf16[64,32,128]{2,1,0:T(8,128)(2,1)} %bitcast.7, bf16[64,32,128]{2,1,0:T(8,128)(2,1)} %bitcast.8, f32[32,8192]{1,0:T(8,128)} %filter_hbm.1, bf16[128,128]{1,0:T(8,128)(2,1)} %constant.12.clone.first_hbm, ...), custom_call_target="tpu_custom_call" | custom-call | tf_op jit(solution)/shard_map/whole/pallas_call | solution.py:379
  60.6 2.6 %finish.1 = (bf16[64,32,128]{2,1,0:T(8,128)(2,1)}, bf16[64,32,128]{2,1,0:T(8,128)(2,1)}, f32[32,8192]{1,0:T(8,128)}) custom-call(bf16[64,4,16,128]{3,2,1,0:T(8,128)(2,1)} %get-tuple-element.8.back_hbm, bf16[64,32,128]{2,1,0:T(8,128)(2,1)} %bitcast.6, f32[32,8192]{1,0:T(8,128)} %get-tuple-element.9.filter_hbm), custom_call_target="tpu_custom_call" | custom-call | tf_op jit(solution)/shard_map/finish/pallas_call | solution.py:424
